TPU v7x, 512 devices: a whole 4x4x16 slice. The times are simulated.
512 devices in a mesh: date: 32 (over z_hi, y, x), col: 16 (over z_lo, core).
Axes of the slice: x: 4, y: 4, z: 16 (z_hi: 2, z_lo: 8; z = z_hi * 8 + z_lo), core: 2. Of those that a mesh axis runs over, the one named last changes fastest.
Arguments:
- slc: float32 [192, 2, 20, 16384], P('date', None, None, 'col'), may hold values from -130 to 130, as said below
- first_row: int32 [192], P('date'), may hold values from 0 to 4
- stop_row: int32 [192], P('date'), may hold values from 16 to 20
- pair_used: int32 [192, 4], P('date'), may hold values 0 or 1
Outputs:
- coherence: float32 [192, 4, 3, 4, 16384], P('date', None, None, None, 'col')
Inputs may be any that keep to these rules, and one draw needn't show every extreme that they name: `slc`: finite values.
All inputs are finite; a program needn't handle non-finite values. No bound on the sum of `pair_used` on one device may be relied on, other than what follows from the above.
Results may differ from a plain program's by a relative error of at most 0.0001.
Values sent between devices are 32-bit elements; how exact they have to be, the bound alone decides.
No kernel may reach another device: no remote copies, remote signals or barrier semaphores. Data moves between devices by JAX's collectives and lax.ppermute only.
A program may use at most 64 MiB of HBM per device.

v0:
```python
import jax
import jax.numpy as jnp
from jax import lax
from jax.sharding import PartitionSpec as P

AZ_LOOKS = 5
RG_LOOKS = 20


def shifted(shard, axis, by):
    count = lax.axis_size(axis)
    pairs = [(i, i + by) for i in range(count) if 0 <= i + by < count]
    return lax.ppermute(shard, axis, pairs)


def extended(block, sides, width):
    for axis, dim in sides:
        count = lax.axis_size(axis)
        forward = [(i, i + 1) for i in range(count - 1)]
        backward = [(target, source) for source, target in forward]
        low = lax.ppermute(
            lax.slice_in_dim(block, block.shape[dim] - width, None, axis=dim), axis, forward
        )
        high = lax.ppermute(lax.slice_in_dim(block, 0, width, axis=dim), axis, backward)
        block = jnp.concatenate([low, block, high], axis=dim)
    return block


def fold_rows(values):
    array_shape = values.shape
    return values.reshape(
        array_shape[:-2] + (array_shape[-2] // AZ_LOOKS, AZ_LOOKS, array_shape[-1])
    ).sum(axis=-2)


def range_sum(padded, col_count):
    running = padded[..., 0:col_count]
    for offset in range(1, RG_LOOKS):
        running = running + padded[..., offset : offset + col_count]
    return running


def pair_products(stacked, block_dates, lag_count):
    own_block = stacked[:block_dates]
    real_list = []
    imag_list = []
    for offset in range(lag_count):
        partner = stacked[offset + 1 : offset + 1 + block_dates]
        real_list.append(own_block[:, 0] * partner[:, 0] + own_block[:, 1] * partner[:, 1])
        imag_list.append(own_block[:, 1] * partner[:, 0] - own_block[:, 0] * partner[:, 1])
    return (jnp.stack(real_list, axis=1), jnp.stack(imag_list, axis=1))


def on_device(slc, first_row, stop_row, pair_used):
    block_dates = slc.shape[0]
    row_count = slc.shape[2]
    col_count = slc.shape[3]
    lag_count = pair_used.shape[1]
    margin = RG_LOOKS // 2
    row_index = lax.broadcasted_iota(jnp.int32, (block_dates, row_count), 1)
    valid = ((row_index >= first_row[:, None]) & (row_index < stop_row[:, None])).astype(
        jnp.float32
    )
    masked = slc * valid[:, None, :, None]
    received = shifted(masked, "date", -1)[:lag_count]
    stacked = jnp.concatenate([masked, received], axis=0)
    padded_stack = extended(stacked, (("col", 3),), margin)
    cross_real, cross_imag = pair_products(padded_stack, block_dates, lag_count)
    cross_real = range_sum(fold_rows(cross_real), col_count)
    cross_imag = range_sum(fold_rows(cross_imag), col_count)
    powers = padded_stack[:, 0] * padded_stack[:, 0] + padded_stack[:, 1] * padded_stack[:, 1]
    powers = range_sum(fold_rows(powers), col_count)
    power_first = powers[:block_dates][:, None]
    power_second = jnp.stack(
        [powers[offset + 1 : offset + 1 + block_dates] for offset in range(lag_count)], axis=1
    )
    scale_down = jnp.sqrt(jnp.maximum(power_first * power_second, 1.0))
    used = pair_used.astype(jnp.float32)[:, :, None, None]
    gamma_real = cross_real * used / scale_down
    gamma_imag = cross_imag * used / scale_down
    magnitude = jnp.sqrt(gamma_real * gamma_real + gamma_imag * gamma_imag)
    return jnp.stack([gamma_real, gamma_imag, magnitude], axis=2)


def solution(mesh):
    return jax.shard_map(
        on_device,
        mesh=mesh,
        in_specs=(P("date", None, None, "col"), P("date"), P("date"), P("date", None)),
        out_specs=P("date", None, None, None, "col"),
        check_vma=False,
    )
```

profile of v0, /device:TPU:62, one launch (start us, length us, event | category | flops | bytes accessed | tf_op | source)
XLA Modules:
  0.0 149.6 jit_solution(3002810155601206968)
XLA Ops:
  0.0 0.8 fusion.11
  0.8 1.6 %broadcast_multiply_fusion = f32[6,2,20,1024]{3,1,2,0:T(2,128)S(1)} fusion(f32[6,2,20,1024]{3,1,2,0:T(2,128)} %param.4, f32[6,20]{1,0:T(8,128)S(1)} %fusion.11), kind=kLoop, calls=%fused_computation.20 | loop fusion | flops 245760 | bytes 1966560 | tf_op jit(solution)/shard_map/mul | solution.py:64
  2.4 2.7 %collective-permute-start = (f32[6,2,20,1024]{3,1,2,0:T(2,128)S(1)}, f32[6,2,20,1024]{3,1,2,0:T(2,128)S(1)}, u32[]{:S(2)}, u32[]{:S(2)}) collective-permute-start(f32[6,2,20,1024]{3,1,2,0:T(2,128)S(1)} %broadcast_multiply_fusion), channel_id=1, source_target_pairs={{16,0},{32,16},{48,32},{64,48},{80,64},{96,80},{112,96},{128,112},... | collective-permute-start | bytes 2949128 | tf_op jit(solution)/shard_map/ppermute | solution.py:13
  5.1 0.0 copy-done.7
  5.1 0.1 copy.17
  5.2 98.7 %collective-permute-done = f32[6,2,20,1024]{3,1,2,0:T(2,128)S(1)} collective-permute-done((f32[6,2,20,1024]{3,1,2,0:T(2,128)S(1)}, f32[6,2,20,1024]{3,1,2,0:T(2,128)S(1)}, u32[]{:S(2)}, u32[]{:S(2)}) %collective-permute-start) | collective-permute-done | bytes 983072 | tf_op jit(solution)/shard_map/ppermute | solution.py:13
  103.9 0.3 fusion.9
  104.3 1.9 %collective-permute-start.2 = (f32[10,2,20,10]{3,1,2,0:T(2,128)S(1)}, f32[10,2,20,10]{3,1,2,0:T(2,128)}, u32[]{:S(2)}, u32[]{:S(2)}) collective-permute-start(f32[10,2,20,10]{3,1,2,0:T(2,128)S(1)} %get-tuple-element.16), channel_id=1, source_target_pairs={{1,0},{2,1},{3,2},{4,3},{5,4},{6,5},{7,6},{8,7},{9,8},{10,9},{11,1... | collective-permute-start | bytes 48008 | tf_op jit(solution)/shard_map/ppermute | solution.py:24
  106.2 2.4 %collective-permute-start.1 = (f32[10,2,20,10]{3,1,2,0:T(2,128)S(1)}, f32[10,2,20,10]{3,1,2,0:T(2,128)}, u32[]{:S(2)}, u32[]{:S(2)}) collective-permute-start(f32[10,2,20,10]{3,1,2,0:T(2,128)S(1)} %get-tuple-element.17), channel_id=1, source_target_pairs={{0,1},{1,2},{2,3},{3,4},{4,5},{5,6},{6,7},{7,8},{8,9},{9,10},{10,1... | collective-permute-start | bytes 48008 | tf_op jit(solution)/shard_map/ppermute | solution.py:21
  108.6 0.9 pad_maximum_fusion
  109.5 0.0 collective-permute-done.2
  109.5 3.9 %collective-permute-done.1 = f32[10,2,20,10]{3,1,2,0:T(2,128)} collective-permute-done((f32[10,2,20,10]{3,1,2,0:T(2,128)S(1)}, f32[10,2,20,10]{3,1,2,0:T(2,128)}, u32[]{:S(2)}, u32[]{:S(2)}) %collective-permute-start.1) | collective-permute-done | bytes 16032 | tf_op jit(solution)/shard_map/ppermute | solution.py:21
  113.4 5.4 %concatenate.9 = f32[10,2,20,1044]{3,1,2,0:T(2,128)S(1)} concatenate(f32[10,2,20,10]{3,1,2,0:T(2,128)} %collective-permute-done.1, f32[10,2,20,1024]{3,1,2,0:T(2,128)S(1)} %pad_maximum_fusion, f32[10,2,20,10]{3,1,2,0:T(2,128)} %collective-permute-done.2), dimensions={3} | concatenate | bytes 3340800 | tf_op jit(solution)/shard_map/concatenate | solution.py:25
  118.8 3.4 %fusion.1 = f32[10,20,1044]{2,1,0:T(8,128)S(1)} fusion(f32[10,2,20,1044]{3,1,2,0:T(2,128)S(1)} %concatenate.9), kind=kLoop, calls=%fused_computation.11 | loop fusion | flops 626400 | bytes 2505600 | tf_op jit(solution)/shard_map/add | solution.py:71
  122.2 4.6 %multiply_subtract_fusion.3 = (f32[6,1,20,1044]{3,1,2,0:T(1,128)S(1)}, f32[6,1,20,1044]{3,1,2,0:T(1,128)}, f32[6,1,20,1044]{3,1,2,0:T(1,128)}, f32[6,1,20,1044]{3,1,2,0:T(1,128)}) fusion(f32[10,2,20,1044]{3,1,2,0:T(2,128)S(1)} %concatenate.9), kind=kLoop, calls=%fused_computation.15 | loop fusion | flops 1503360 | bytes 6013440 | tf_op jit(solution)/shard_map/sub | solution.py:50
  126.8 4.7 %multiply_subtract_fusion.2 = (f32[6,1,20,1044]{3,1,2,0:T(1,128)}, f32[6,1,20,1044]{3,1,2,0:T(1,128)}, f32[6,1,20,1044]{3,1,2,0:T(1,128)}, f32[6,1,20,1044]{3,1,2,0:T(1,128)}) fusion(f32[10,2,20,1044]{3,1,2,0:T(2,128)S(1)} %concatenate.9), kind=kLoop, calls=%fused_computation.14 | loop fusion | flops 1503360 | bytes 6013440 | tf_op jit(solution)/shard_map/sub | solution.py:50
  131.5 0.1 add.225
  131.7 0.5 reduce_sum.28
  132.2 0.0 copy-start.1
  132.2 0.0 copy-start.2
  132.2 0.0 copy-start.3
  132.2 0.0 copy-start.4
  132.3 1.7 %slice_add_fusion.38 = f32[10,4,1024]{2,1,0:T(4,128)S(1)} fusion(f32[10,4,1044]{2,1,0:T(4,128)S(1)} %reduce_sum.28), kind=kLoop, calls=%fused_computation.69 | loop fusion | flops 778240 | bytes 3440640 | tf_op jit(solution)/shard_map/add | solution.py:39
  133.9 0.1 fusion.14
  134.0 0.1 stack.65
  134.1 0.1 copy.20
  134.2 0.1 copy.19
  134.3 0.1 copy.18
  134.5 4.9 %maximum_reduce_fusion = (f32[6,4,4,1044]{3,1,2,0:T(4,128)S(1)}, f32[6,4,4,1044]{3,1,2,0:T(4,128)S(1)}) fusion(f32[6,1,4,5,1044]{4,1,3,2,0:T(1,128)S(1)} %bitcast.25, f32[6,1,4,5,1044]{4,1,3,2,0:T(1,128)S(1)} %bitcast.20, f32[6,1,4,5,1044]{4,1,3,2,0:T(1,128)S(1)} %bitcast.23, f32[6,1,4,5,1044]{4,1,3,2,0:T(1,128)S(1)} %bitcast.24, ...), kind=kLoop, calls=%fused_computation | loop fusion | flops 3808512 | bytes 4810752 | tf_op jit(solution)/shard_map/reduce_sum | solution.py:33
  139.4 8.0 %sqrt_bitcast_fusion = (f32[6,4,1,4,1024]{4,1,3,0,2:T(4,128)S(1)}, f32[6,4,4,1024]{3,1,2,0:T(4,128)S(1)}, f32[6,4,4,1024]{3,1,2,0:T(4,128)S(1)}) fusion(f32[6,1,4,1024]{3,1,2,0:T(1,128)S(1)} %stack.65, f32[6,1,4,1024]{3,1,2,0:T(1,128)S(1)} %copy.20, f32[6,1,4,1024]{3,1,2,0:T(1,128)S(1)} %copy.19, f32[6,1,4,1024]{3,1,2,0:T(1,128)S(1)} %copy.18, ...), kind=kLoop, calls=%fused_computation.66 | loop fusion | flops 4915200 | bytes 17399904 | tf_op jit(solution)/shard_map/stack | solution.py:82
  147.4 0.4 pad_maximum_fusion.1
  147.8 1.8 %copy.21 = f32[6,4,3,4,1024]{4,3,2,1,0:T(4,128)} copy(f32[6,4,3,4,1024]{4,1,3,0,2:T(4,128)S(1)} %pad_maximum_fusion.1) | data formatting | bytes 2359296 | tf_op jit(solution)/shard_map/stack | solution.py:82
  (13 shorter events, 0.1 us)
Async XLA Ops:
  0.0 5.1 %copy-start.7 = (s32[6,4]{0,1:T(4,128)S(1)}, s32[6,4]{0,1:T(4,128)}, u32[]{:S(2)}) copy-start(s32[6,4]{0,1:T(4,128)} %param.7) | copy-start | bytes 292
  2.4 101.5 %collective-permute-start = (f32[6,2,20,1024]{3,1,2,0:T(2,128)S(1)}, f32[6,2,20,1024]{3,1,2,0:T(2,128)S(1)}, u32[]{:S(2)}, u32[]{:S(2)}) collective-permute-start(f32[6,2,20,1024]{3,1,2,0:T(2,128)S(1)} %broadcast_multiply_fusion), channel_id=1, source_target_pairs={{16,0},{32,16},{48,32},{64,48},{80,64},{96,80},{112,96},{128,112},... | collective-permute-start | bytes 2949128 | tf_op jit(solution)/shard_map/ppermute | solution.py:13
  104.3 5.2 %collective-permute-start.2 = (f32[10,2,20,10]{3,1,2,0:T(2,128)S(1)}, f32[10,2,20,10]{3,1,2,0:T(2,128)}, u32[]{:S(2)}, u32[]{:S(2)}) collective-permute-start(f32[10,2,20,10]{3,1,2,0:T(2,128)S(1)} %get-tuple-element.16), channel_id=1, source_target_pairs={{1,0},{2,1},{3,2},{4,3},{5,4},{6,5},{7,6},{8,7},{9,8},{10,9},{11,1... | collective-permute-start | bytes 48008 | tf_op jit(solution)/shard_map/ppermute | solution.py:24
  106.2 7.2 %collective-permute-start.1 = (f32[10,2,20,10]{3,1,2,0:T(2,128)S(1)}, f32[10,2,20,10]{3,1,2,0:T(2,128)}, u32[]{:S(2)}, u32[]{:S(2)}) collective-permute-start(f32[10,2,20,10]{3,1,2,0:T(2,128)S(1)} %get-tuple-element.17), channel_id=1, source_target_pairs={{0,1},{1,2},{2,3},{3,4},{4,5},{5,6},{6,7},{7,8},{8,9},{9,10},{10,1... | collective-permute-start | bytes 48008 | tf_op jit(solution)/shard_map/ppermute | solution.py:21
  132.2 2.3 %copy-start = (f32[6,1,20,1044]{3,1,2,0:T(1,128)S(1)}, f32[6,1,20,1044]{3,1,2,0:T(1,128)}, u32[]{:S(2)}) copy-start(f32[6,1,20,1044]{3,1,2,0:T(1,128)} %get-tuple-element.9) | copy-start | bytes 1503364
  132.2 2.3 %copy-start.1 = (f32[6,1,20,1044]{3,1,2,0:T(1,128)S(1)}, f32[6,1,20,1044]{3,1,2,0:T(1,128)}, u32[]{:S(2)}) copy-start(f32[6,1,20,1044]{3,1,2,0:T(1,128)} %get-tuple-element.10) | copy-start | bytes 1503364
  132.2 2.3 %copy-start.2 = (f32[6,1,20,1044]{3,1,2,0:T(1,128)S(1)}, f32[6,1,20,1044]{3,1,2,0:T(1,128)}, u32[]{:S(2)}) copy-start(f32[6,1,20,1044]{3,1,2,0:T(1,128)} %get-tuple-element.11) | copy-start | bytes 1503364
  132.2 2.3 %copy-start.3 = (f32[6,1,20,1044]{3,1,2,0:T(1,128)S(1)}, f32[6,1,20,1044]{3,1,2,0:T(1,128)}, u32[]{:S(2)}) copy-start(f32[6,1,20,1044]{3,1,2,0:T(1,128)} %get-tuple-element.12) | copy-start | bytes 1503364
  132.2 2.2 %copy-start.4 = (f32[6,1,20,1044]{3,1,2,0:T(1,128)S(1)}, f32[6,1,20,1044]{3,1,2,0:T(1,128)}, u32[]{:S(2)}) copy-start(f32[6,1,20,1044]{3,1,2,0:T(1,128)} %get-tuple-element.13) | copy-start | bytes 1503364
  132.3 2.2 %copy-start.5 = (f32[6,1,20,1044]{3,1,2,0:T(1,128)S(1)}, f32[6,1,20,1044]{3,1,2,0:T(1,128)}, u32[]{:S(2)}) copy-start(f32[6,1,20,1044]{3,1,2,0:T(1,128)} %get-tuple-element.14) | copy-start | bytes 1503364
  132.3 2.2 %copy-start.6 = (f32[6,1,20,1044]{3,1,2,0:T(1,128)S(1)}, f32[6,1,20,1044]{3,1,2,0:T(1,128)}, u32[]{:S(2)}) copy-start(f32[6,1,20,1044]{3,1,2,0:T(1,128)} %get-tuple-element.15) | copy-start | bytes 1503364
where the time goes:
time: 150 us
  waiting for transfers between devices  103 us (69%)
  other arithmetic  31.8 us (21%)
  local copies, waits for them, and re-layouts  7.99 us (5%)
  starting transfers between devices  7.07 us (5%)
    ppermute x1, waiting for transfers between devices, shifted(): return lax.ppermute(shard, axis, pairs)  98.7 us
    sub x2, other arithmetic, pair_products(): own_block[:, 1] * partner[:, 0] - own_block[:, 0] * partner[:, 1]  9.37 us
    another operation x2, other arithmetic, on_device(): return jnp.stack([gamma_real, gamma_imag, magnitude], axis=2)  8.43 us
    concatenate x1, local copies, waits for them, and re-layouts, extended(): block = jnp.concatenate([low, block, high], axis=dim)  5.42 us
    reduce_sum x2, other arithmetic, fold_rows(): return values.reshape(array_shape[:-2] + (array_shape[-2] // AZ_LOOKS, AZ...  5.38 us
    ppermute x1, waiting for transfers between devices, extended(): lax.ppermute(lax.slice_in_dim(block, block.shape[dim] - width, None, axis...  3.88 us
    add x1, other arithmetic, on_device(): padded_stack[:, 0] * padded_stack[:, 0]  3.37 us
  transfers between devices with their start and end apart: 3, of which 2 were waited for; matrix products, arithmetic and copies ran while one was open for 1% of the time, Pallas kernels for 0%

commit v1 on v0

v1 whole, which is shorter than its diff:
```python
import functools

import jax
import jax.numpy as jnp
from jax import lax
from jax.experimental import pallas as pl
from jax.experimental.pallas import tpu as pltpu
from jax.sharding import PartitionSpec as P

AZ = 5
LAG = 4
DATES = 6
LOOKS = 4
COLS = 1024
LANES = 128
CHUNKS = COLS // LANES
WIDE = COLS + LANES
AXES = ("date", "col")

PIECES = (7, 7, 6)
COLUMN_SETS = (
    ((0, 0), (3, 0), (0, 3)),
    ((3, 3), (1, 0), (0, 1)),
    ((2, 3), (3, 2), (1, 3)),
    ((3, 1), (2, 0), (0, 2)),
)
SOURCE_XY = (0, 0)
TARGET_XY = (3, 3)

INNER_PAIRS = [(i, k) for i in range(DATES) for k in range(LAG) if i + k + 1 < DATES]
OUTER_PAIRS = [(i, k) for i in range(DATES) for k in range(LAG) if i + k + 1 >= DATES]

VMEM = pl.BlockSpec(memory_space=pltpu.VMEM)
SMEM = pl.BlockSpec(memory_space=pltpu.SMEM)
ANY = pl.BlockSpec(memory_space=pl.ANY)


def lane_roll(x, by):
    return pltpu.roll(x, by % x.shape[-1], axis=x.ndim - 1)


def half_swap(x):
    return pltpu.roll(x, LOOKS, axis=0)


def window(x):
    s2 = x + lane_roll(x, -1)
    s4 = s2 + lane_roll(s2, 2)
    s8 = s4 + lane_roll(s4, -4)
    s16 = s8 + lane_roll(s8, 8)
    return (s16 + lane_roll(s4, -8))[:, :COLS]


def prepare(slc, first, stop, *refs):
    own_low, own_high, edge_low, edge_high = refs[:4]
    pieces = refs[4 : 4 + len(PIECES)]
    buf, sems = refs[4 + len(PIECES) :]

    def copy(j):
        return pltpu.make_async_copy(
            slc.at[:, :, :, pl.ds(j * LANES, LANES)], buf.at[j], sems.at[j]
        )

    for j in range(CHUNKS):
        copy(j).start()
    row = AZ * lax.broadcasted_iota(jnp.int32, (LOOKS, LANES), 0)
    starts = [sum(PIECES[:n]) for n in range(len(PIECES))]
    for j in range(CHUNKS):
        copy(j).wait()
        lanes = slice(j * LANES, (j + 1) * LANES)
        for d in range(DATES):
            for q in range(AZ):
                keep = (row + q >= first[d]) & (row + q < stop[d])
                tile = []
                for part in range(2):
                    value = buf[j, d, part, pl.ds(q, LOOKS, stride=AZ), :]
                    tile.append(jnp.where(keep, value, 0.0))
                tile = jnp.concatenate(tile, axis=0)
                if d < LAG:
                    own_low[d, q, :, lanes] = tile
                    unit = d * AZ + q
                    for start, size, piece in zip(starts, PIECES, pieces):
                        if start <= unit < start + size:
                            piece[unit - start, :, lanes] = tile
                else:
                    own_high[d - LAG, q, :, lanes] = tile
                if j == 0:
                    edge_low[d, q] = tile
                if j == CHUNKS - 1:
                    edge_high[d, q] = tile


def products(a, b, b_swapped):
    straight = a[0] * b[0]
    crossed = a[0] * b_swapped[0]
    for q in range(1, AZ):
        straight = straight + a[q] * b[q]
        crossed = crossed + a[q] * b_swapped[q]
    upper = lax.broadcasted_iota(jnp.int32, straight.shape, 0) < LOOKS
    return jnp.where(
        upper, straight + half_swap(straight), crossed - half_swap(crossed)
    )


def power_of(a):
    total = a[0] * a[0]
    for q in range(1, AZ):
        total = total + a[q] * a[q]
    return total + half_swap(total)


def write_pair(store, cross, power_first, power_second, used):
    gamma = window(cross) * (
        used * lax.rsqrt(jnp.maximum(power_first * power_second, 1.0))
    )
    square = gamma * gamma
    magnitude = jnp.sqrt(square + half_swap(square))
    store(0, gamma[:LOOKS])
    store(1, gamma[LOOKS:])
    store(2, magnitude[:LOOKS])


def inner(own_low, own_high, right, left, used, out, power, packed, sums, powers):
    lane = lax.broadcasted_iota(jnp.int32, (8, LANES), 1)

    def chunk(tiles, lanes):
        swapped = [None] + [[half_swap(t) for t in tiles[d]] for d in range(1, DATES)]
        for d in range(DATES):
            powers[d, :, lanes] = power_of(tiles[d])
        for n, (i, k) in enumerate(INNER_PAIRS):
            j = i + k + 1
            sums[n, :, lanes] = products(tiles[i], tiles[j], swapped[j])

    halo = [
        [jnp.where(lane < LANES // 2, right[d, q], left[d, q]) for q in range(AZ)]
        for d in range(DATES)
    ]
    for q in range(AZ):
        merged = halo[0][q]
        for d in range(1, LAG):
            here = (lane >= 32 * d - 16) & (lane < 32 * d + 16)
            merged = jnp.where(here, lane_roll(halo[d][q], 32 * d), merged)
        packed[q] = merged
    chunk(halo, pl.ds(COLS, LANES))

    @pl.loop(0, CHUNKS)
    def _(c):
        lanes = pl.ds(pl.multiple_of(c * LANES, LANES), LANES)
        chunk(
            [[own_low[d, q, :, lanes] for q in range(AZ)] for d in range(LAG)]
            + [[own_high[d, q, :, lanes] for q in range(AZ)] for d in range(DATES - LAG)],
            lanes,
        )

    for d in range(DATES):
        power[d] = window(powers[d])
    for n, (i, k) in enumerate(INNER_PAIRS):

        def store(m, value, i=i, k=k):
            out[i, k, m] = value

        write_pair(
            store,
            sums[n],
            power[i],
            power[i + k + 1],
            used[i, k].astype(jnp.float32),
        )


def outer(own_low, own_high, right, left, power, used, received, packed, *refs):
    count = len(PIECES)
    pieces = refs[:count]
    out, sums, powers, staged, sems = refs[count + 1 :]
    lane = lax.broadcasted_iota(jnp.int32, (8, LANES), 1)
    starts = [sum(PIECES[:n]) for n in range(count)]
    firsts = sorted({i for i, _ in OUTER_PAIRS})

    def chunk(mine, theirs, lanes):
        swapped = [[half_swap(t) for t in tiles] for tiles in theirs]
        for d in range(LAG):
            powers[d, :, lanes] = power_of(theirs[d])
        for n, (i, k) in enumerate(OUTER_PAIRS):
            j = i + k + 1 - DATES
            sums[n, :, lanes] = products(mine[i], theirs[j], swapped[j])

    chunk(
        {
            d: [jnp.where(lane < LANES // 2, right[d, q], left[d, q]) for q in range(AZ)]
            for d in firsts
        },
        [[lane_roll(packed[q], -32 * d) for q in range(AZ)] for d in range(LAG)],
        pl.ds(COLS, LANES),
    )

    @pl.loop(0, CHUNKS)
    def _(c):
        lanes = pl.ds(pl.multiple_of(c * LANES, LANES), LANES)
        mine = {}
        for d in firsts:
            ref, at = (own_low, d) if d < LAG else (own_high, d - LAG)
            mine[d] = [ref[at, q, :, lanes] for q in range(AZ)]
        theirs = []
        for d in range(LAG):
            tiles = []
            for q in range(AZ):
                unit = d * AZ + q
                tile = received[d, q, :, lanes]
                for start, size, piece in zip(starts, PIECES, pieces):
                    if start <= unit < start + size:
                        tile = tile + piece[unit - start, :, lanes]
                tiles.append(tile)
            theirs.append(tiles)
        chunk(mine, theirs, lanes)

    their_power = [window(powers[d]) for d in range(LAG)]
    copies = []
    for n, (i, k) in enumerate(OUTER_PAIRS):

        def store(m, value, n=n):
            staged[n, m] = value

        write_pair(
            store,
            sums[n],
            power[i],
            their_power[i + k + 1 - DATES],
            used[i, k].astype(jnp.float32),
        )
        copies.append(pltpu.make_async_copy(staged.at[n], out.at[i, k], sems.at[n]))
        copies[-1].start()
    for copy in copies:
        copy.wait()


def far_permutes():
    def flat(x, y, z, core):
        return ((z // 8) * 16 + y * 4 + x) * 16 + (z % 8) * 2 + core

    scatter = [[] for _ in PIECES]
    gather = [[] for _ in PIECES]
    for z in range(8):
        for core in range(2):
            for n, (x, y) in enumerate(COLUMN_SETS[z // 2][: len(PIECES)]):
                relay = flat(x, y, 8 + z, core)
                scatter[n].append((flat(*SOURCE_XY, 8 + z, core), relay))
                gather[n].append((relay, flat(*TARGET_XY, z, core)))
    return scatter, gather


def f32(*shape):
    return jax.ShapeDtypeStruct(shape, jnp.float32)


def on_device(slc, first_row, stop_row, pair_used):
    rest = DATES - LAG
    own_low, own_high, edge_low, edge_high, *pieces = pl.pallas_call(
        prepare,
        out_shape=[
            f32(LAG, AZ, 8, COLS),
            f32(rest, AZ, 8, COLS),
            f32(DATES, AZ, 8, LANES),
            f32(DATES, AZ, 8, LANES),
        ]
        + [f32(size, 8, COLS) for size in PIECES],
        in_specs=[ANY, SMEM, SMEM],
        out_specs=[VMEM] * (4 + len(PIECES)),
        scratch_shapes=[
            pltpu.VMEM((CHUNKS, DATES, 2, AZ * LOOKS, LANES), jnp.float32),
            pltpu.SemaphoreType.DMA((CHUNKS,)),
        ],
        name="prepare",
    )(slc, first_row, stop_row)

    def permute(value, pairs):
        return lax.ppermute(value, AXES, pairs)

    near = [
        (d * 16 + c, (d - 1) * 16 + c) for d in range(1, 32) if d != 16 for c in range(16)
    ]
    far = [(16 * 16 + c, 15 * 16 + c) for c in range(16)]
    to_right = [(d * 16 + c, d * 16 + c + 1) for d in range(32) for c in range(15)]
    to_left = [(b, a) for a, b in to_right]
    scatter, gather = far_permutes()
    scattered = [permute(piece, pairs) for piece, pairs in zip(pieces, scatter)]
    received = permute(own_low, near)
    left = permute(edge_high, to_right)
    right = permute(edge_low, to_left)
    gathered = [permute(piece, pairs) for piece, pairs in zip(scattered, gather)]

    out_shape = f32(DATES, LAG, 3, LOOKS, COLS)
    out, power, packed = pl.pallas_call(
        inner,
        out_shape=[out_shape, f32(DATES, 8, COLS), f32(AZ, 8, LANES)],
        in_specs=[VMEM] * 4 + [SMEM],
        out_specs=[VMEM] * 3,
        scratch_shapes=[
            pltpu.VMEM((len(INNER_PAIRS), 8, WIDE), jnp.float32),
            pltpu.VMEM((DATES, 8, WIDE), jnp.float32),
        ],
        name="inner",
    )(own_low, own_high, right, left, pair_used)
    their_packed = permute(packed, near + far)
    count = len(PIECES)
    return pl.pallas_call(
        outer,
        out_shape=out_shape,
        in_specs=[VMEM] * 5 + [SMEM] + [VMEM] * (2 + count) + [ANY],
        out_specs=ANY,
        input_output_aliases={8 + count: 0},
        scratch_shapes=[
            pltpu.VMEM((len(OUTER_PAIRS), 8, WIDE), jnp.float32),
            pltpu.VMEM((LAG, 8, WIDE), jnp.float32),
            pltpu.VMEM((len(OUTER_PAIRS), 3, LOOKS, COLS), jnp.float32),
            pltpu.SemaphoreType.DMA((len(OUTER_PAIRS),)),
        ],
        name="outer",
    )(own_low, own_high, right, left, power, pair_used, received, their_packed, *gathered, out)


def solution(mesh):
    return jax.shard_map(
        on_device,
        mesh=mesh,
        in_specs=(P("date", None, None, "col"), P("date"), P("date"), P("date", None)),
        out_specs=P("date", None, None, None, "col"),
        check_vma=False,
    )
```

time: 150 us -> 59.5 us (0.40)
  the two profiles are of different devices: /device:TPU:62 before, /device:TPU:158 now
where the time goes in v1:
time: 59.5 us; the launch traced here: 59.1 us
  waiting for transfers between devices  23.7 us (40%)
  starting transfers between devices  15.2 us (26%)
  Pallas kernels  15.1 us (25%)
  local copies, waits for them, and re-layouts  4.91 us (8%)
    ppermute x10, waiting for transfers between devices, permute(): return lax.ppermute(value, AXES, pairs)  23.7 us
    ppermute x10, starting transfers between devices, permute(): return lax.ppermute(value, AXES, pairs)  15.2 us
    pallas_call x1, Pallas kernels, on_device(): pl.pallas_call(inner, out_shape=[out_shape, f32(DATES, 8, COLS), f32(AZ,...  6.54 us
    pallas_call x1, Pallas kernels, on_device(): pl.pallas_call(outer, out_shape=out_shape, in_specs=[VMEM] * 5 + [SMEM] +...  5.25 us
    unnamed x18, local copies, waits for them, and re-layouts  4.91 us
    pallas_call x1, Pallas kernels, on_device(): pl.pallas_call(prepare, out_shape=[f32(LAG, AZ, 8, COLS), f32(rest, AZ, 8...  3.33 us
  transfers between devices with their start and end apart: 10, of which 2 were waited for; matrix products, arithmetic and copies ran while one was open for 1% of the time, Pallas kernels for 11%

profile of v1, /device:TPU:158, one launch (start us, length us, event | category | flops | bytes accessed | tf_op | source)
XLA Modules:
  0.0 59.1 jit_solution(15099499715426140311)
XLA Ops:
  0.0 2.5 %copy.6.slc = f32[6,2,20,1024]{3,2,1,0:T(8,128)} copy(f32[6,2,20,1024]{3,1,2,0:T(2,128)} %param.4) | data formatting | bytes 1966080 | tf_op args[0]
  2.5 3.3 %prepare.1 = (f32[4,5,8,1024]{3,2,1,0:T(8,128)}, f32[2,5,8,1024]{3,2,1,0:T(8,128)}, f32[6,5,8,128]{3,2,1,0:T(8,128)}, f32[6,5,8,128]{3,2,1,0:T(8,128)}, f32[7,8,...) custom-call(f32[6,2,20,1024]{3,2,1,0:T(8,128)} %copy.6.slc, s32[6]{0:T(128)} %first.1, s32[6]{0:T(128)} %stop.1), custom_call_target="tpu_custom_call" | custom-call | tf_op jit(solution)/shard_map/prepare/pallas_call | solution.py:257
  5.9 2.8 %collective-permute-start.2 = (f32[4,5,8,1024]{3,2,1,0:T(8,128)}, f32[4,5,8,1024]{3,2,1,0:T(8,128)S(1)}, u32[]{:S(2)}, u32[]{:S(2)}) collective-permute-start(f32[4,5,8,1024]{3,2,1,0:T(8,128)} %get-tuple-element.15.own_low), channel_id=1, source_target_pairs={{16,0},{17,1},{18,2},{19,3},{20,4},{21,5},{22,6},{23,7},{24,8},{25... | collective-permute-start | bytes 1966088 | tf_op jit(solution)/shard_map/ppermute | solution.py:276
  8.7 0.7 %collective-permute-start.4 = (f32[7,8,1024]{2,1,0:T(8,128)}, f32[7,8,1024]{2,1,0:T(8,128)S(1)}, u32[]{:S(2)}, u32[]{:S(2)}) collective-permute-start(f32[7,8,1024]{2,1,0:T(8,128)} %get-tuple-element.21), channel_id=1, source_target_pairs={{256,256},{257,257},{258,258},{259,259},{260,500},{261,501},{262,5... | collective-permute-start | bytes 688136 | tf_op jit(solution)/shard_map/ppermute | solution.py:276
  9.3 0.7 %collective-permute-start.6 = (f32[7,8,1024]{2,1,0:T(8,128)}, f32[7,8,1024]{2,1,0:T(8,128)S(1)}, u32[]{:S(2)}, u32[]{:S(2)}) collective-permute-start(f32[7,8,1024]{2,1,0:T(8,128)} %get-tuple-element.22), channel_id=1, source_target_pairs={{256,304},{257,305},{258,306},{259,307},{260,276},{261,277},{262,2... | collective-permute-start | bytes 688136 | tf_op jit(solution)/shard_map/ppermute | solution.py:276
  10.0 0.7 %collective-permute-start.8 = (f32[6,8,1024]{2,1,0:T(8,128)}, f32[6,8,1024]{2,1,0:T(8,128)S(1)}, u32[]{:S(2)}, u32[]{:S(2)}) collective-permute-start(f32[6,8,1024]{2,1,0:T(8,128)} %get-tuple-element.23), channel_id=1, source_target_pairs={{256,448},{257,449},{258,450},{259,451},{260,324},{261,325},{262,3... | collective-permute-start | bytes 589832 | tf_op jit(solution)/shard_map/ppermute | solution.py:276
  10.7 1.9 %collective-permute-start = (f32[6,5,8,128]{3,2,1,0:T(8,128)}, f32[6,5,8,128]{3,2,1,0:T(8,128)S(1)}, u32[]{:S(2)}, u32[]{:S(2)}) collective-permute-start(f32[6,5,8,128]{3,2,1,0:T(8,128)} %get-tuple-element.17), channel_id=1, source_target_pairs={{1,0},{2,1},{3,2},{4,3},{5,4},{6,5},{7,6},{8,7},{9,8},{10,9},{11,1... | collective-permute-start | bytes 368648 | tf_op jit(solution)/shard_map/ppermute | solution.py:276
  12.6 0.0 collective-permute-done.4
  12.6 1.3 %collective-permute-start.5 = (f32[7,8,1024]{2,1,0:T(8,128)S(1)}, f32[7,8,1024]{2,1,0:T(8,128)S(1)}, u32[]{:S(2)}, u32[]{:S(2)}) collective-permute-start(f32[7,8,1024]{2,1,0:T(8,128)S(1)} %collective-permute-done.4), channel_id=1, source_target_pairs={{256,240},{257,241},{258,242},{259,243},{500,244},{501,245},{502,2... | collective-permute-start | bytes 688136 | tf_op jit(solution)/shard_map/ppermute | solution.py:276
  13.9 0.0 collective-permute-done.6
  14.0 1.3 %collective-permute-start.7 = (f32[7,8,1024]{2,1,0:T(8,128)S(1)}, f32[7,8,1024]{2,1,0:T(8,128)S(1)}, u32[]{:S(2)}, u32[]{:S(2)}) collective-permute-start(f32[7,8,1024]{2,1,0:T(8,128)S(1)} %collective-permute-done.6), channel_id=1, source_target_pairs={{304,240},{305,241},{306,242},{307,243},{276,244},{277,245},{278,2... | collective-permute-start | bytes 688136 | tf_op jit(solution)/shard_map/ppermute | solution.py:276
  15.3 0.0 collective-permute-done.8
  15.3 1.3 %collective-permute-start.9 = (f32[6,8,1024]{2,1,0:T(8,128)S(1)}, f32[6,8,1024]{2,1,0:T(8,128)S(1)}, u32[]{:S(2)}, u32[]{:S(2)}) collective-permute-start(f32[6,8,1024]{2,1,0:T(8,128)S(1)} %collective-permute-done.8), channel_id=1, source_target_pairs={{448,240},{449,241},{450,242},{451,243},{324,244},{325,245},{326,2... | collective-permute-start | bytes 589832 | tf_op jit(solution)/shard_map/ppermute | solution.py:276
  16.6 0.0 collective-permute-done.right
  16.6 2.7 %collective-permute-start.1 = (f32[6,5,8,128]{3,2,1,0:T(8,128)}, f32[6,5,8,128]{3,2,1,0:T(8,128)S(1)}, u32[]{:S(2)}, u32[]{:S(2)}) collective-permute-start(f32[6,5,8,128]{3,2,1,0:T(8,128)} %get-tuple-element.18), channel_id=1, source_target_pairs={{0,1},{1,2},{2,3},{3,4},{4,5},{5,6},{6,7},{7,8},{8,9},{9,10},{10,1... | collective-permute-start | bytes 368648 | tf_op jit(solution)/shard_map/ppermute | solution.py:276
  19.3 0.7 %copy.7.used = s32[6,4]{1,0:T(8,128)} copy(s32[6,4]{0,1:T(4,128)S(1)} %copy-done.7) | data formatting | bytes 192 | tf_op args[3]
  20.0 4.2 %collective-permute-done.1.left = f32[6,5,8,128]{3,2,1,0:T(8,128)S(1)} collective-permute-done((f32[6,5,8,128]{3,2,1,0:T(8,128)}, f32[6,5,8,128]{3,2,1,0:T(8,128)S(1)}, u32[]{:S(2)}, u32[]{:S(2)}) %collective-permute-start.1) | collective-permute-done | bytes 122912 | tf_op jit(solution)/shard_map/ppermute | solution.py:276
  24.2 0.6 %copy-done.2 = f32[6,5,8,128]{3,2,1,0:T(8,128)} copy-done((f32[6,5,8,128]{3,2,1,0:T(8,128)}, f32[6,5,8,128]{3,2,1,0:T(8,128)S(1)}, u32[]{:S(2)}) %copy-start.2) | copy-done | bytes 122904
  24.9 6.5 %inner.1 = (f32[6,4,3,4,1024]{4,3,2,1,0:T(4,128)}, f32[6,8,1024]{2,1,0:T(8,128)}, f32[5,8,128]{2,1,0:T(8,128)}) custom-call(f32[4,5,8,1024]{3,2,1,0:T(8,128)} %get-tuple-element.15.own_low, f32[2,5,8,1024]{3,2,1,0:T(8,128)} %get-tuple-element.16.own_high, f32[6,5,8,128]{3,2,1,0:T(8,128)} %copy-done.1, f32[6,5,8,128]{3,2,1,0:T(8,128)} %copy-done.2, ...), custom_call_target="tpu_custom_call" | custom-call | tf_op jit(solution)/shard_map/inner/pallas_call | solution.py:292
  31.4 1.9 %collective-permute-start.3 = (f32[5,8,128]{2,1,0:T(8,128)}, f32[5,8,128]{2,1,0:T(8,128)S(1)}, u32[]{:S(2)}, u32[]{:S(2)}) collective-permute-start(f32[5,8,128]{2,1,0:T(8,128)} %get-tuple-element.20), channel_id=1, source_target_pairs={{16,0},{17,1},{18,2},{19,3},{20,4},{21,5},{22,6},{23,7},{24,8},{25... | collective-permute-start | bytes 61448 | tf_op jit(solution)/shard_map/ppermute | solution.py:276
  33.3 19.4 %collective-permute-done.3.packed = f32[5,8,128]{2,1,0:T(8,128)S(1)} collective-permute-done((f32[5,8,128]{2,1,0:T(8,128)}, f32[5,8,128]{2,1,0:T(8,128)S(1)}, u32[]{:S(2)}, u32[]{:S(2)}) %collective-permute-start.3) | collective-permute-done | bytes 20512 | tf_op jit(solution)/shard_map/ppermute | solution.py:276
  52.8 0.0 collective-permute-done.9.refs_2_
  52.8 0.0 collective-permute-done.5.refs_0_
  52.8 0.0 copy-start.3
  52.8 0.0 collective-permute-done.7.refs_1_
  52.8 0.0 collective-permute-done.2.received
  52.8 0.5 copy-done.6
  53.4 0.1 copy-done.5
  53.4 0.1 copy-done.3
  53.5 0.1 copy-done.4
  53.6 0.2 copy-done
  53.9 5.3 %outer.1 = f32[6,4,3,4,1024]{4,3,2,1,0:T(4,128)} custom-call(f32[4,5,8,1024]{3,2,1,0:T(8,128)} %get-tuple-element.15.own_low, f32[2,5,8,1024]{3,2,1,0:T(8,128)} %get-tuple-element.16.own_high, f32[6,5,8,128]{3,2,1,0:T(8,128)} %copy-done.1, f32[6,5,8,128]{3,2,1,0:T(8,128)} %copy-done.2, ...), custom_call_target="tpu_custom_call", output_to_operand_aliasing={{}: (11, {})} | custom-call | tf_op jit(solution)/shard_map/outer/pallas_call | solution.py:305
  (9 shorter events, 0.0 us)
Async XLA Ops:
  0.0 19.3 %copy-start.7 = (s32[6,4]{0,1:T(4,128)S(1)}, s32[6,4]{0,1:T(4,128)}, u32[]{:S(2)}) copy-start(s32[6,4]{0,1:T(4,128)} %param.7) | copy-start | bytes 292
  5.9 46.9 %collective-permute-start.2 = (f32[4,5,8,1024]{3,2,1,0:T(8,128)}, f32[4,5,8,1024]{3,2,1,0:T(8,128)S(1)}, u32[]{:S(2)}, u32[]{:S(2)}) collective-permute-start(f32[4,5,8,1024]{3,2,1,0:T(8,128)} %get-tuple-element.15.own_low), channel_id=1, source_target_pairs={{16,0},{17,1},{18,2},{19,3},{20,4},{21,5},{22,6},{23,7},{24,8},{25... | collective-permute-start | bytes 1966088 | tf_op jit(solution)/shard_map/ppermute | solution.py:276
  8.7 4.0 %collective-permute-start.4 = (f32[7,8,1024]{2,1,0:T(8,128)}, f32[7,8,1024]{2,1,0:T(8,128)S(1)}, u32[]{:S(2)}, u32[]{:S(2)}) collective-permute-start(f32[7,8,1024]{2,1,0:T(8,128)} %get-tuple-element.21), channel_id=1, source_target_pairs={{256,256},{257,257},{258,258},{259,259},{260,500},{261,501},{262,5... | collective-permute-start | bytes 688136 | tf_op jit(solution)/shard_map/ppermute | solution.py:276
  9.3 4.6 %collective-permute-start.6 = (f32[7,8,1024]{2,1,0:T(8,128)}, f32[7,8,1024]{2,1,0:T(8,128)S(1)}, u32[]{:S(2)}, u32[]{:S(2)}) collective-permute-start(f32[7,8,1024]{2,1,0:T(8,128)} %get-tuple-element.22), channel_id=1, source_target_pairs={{256,304},{257,305},{258,306},{259,307},{260,276},{261,277},{262,2... | collective-permute-start | bytes 688136 | tf_op jit(solution)/shard_map/ppermute | solution.py:276
  10.0 5.2 %collective-permute-start.8 = (f32[6,8,1024]{2,1,0:T(8,128)}, f32[6,8,1024]{2,1,0:T(8,128)S(1)}, u32[]{:S(2)}, u32[]{:S(2)}) collective-permute-start(f32[6,8,1024]{2,1,0:T(8,128)} %get-tuple-element.23), channel_id=1, source_target_pairs={{256,448},{257,449},{258,450},{259,451},{260,324},{261,325},{262,3... | collective-permute-start | bytes 589832 | tf_op jit(solution)/shard_map/ppermute | solution.py:276
  10.7 5.9 %collective-permute-start = (f32[6,5,8,128]{3,2,1,0:T(8,128)}, f32[6,5,8,128]{3,2,1,0:T(8,128)S(1)}, u32[]{:S(2)}, u32[]{:S(2)}) collective-permute-start(f32[6,5,8,128]{3,2,1,0:T(8,128)} %get-tuple-element.17), channel_id=1, source_target_pairs={{1,0},{2,1},{3,2},{4,3},{5,4},{6,5},{7,6},{8,7},{9,8},{10,9},{11,1... | collective-permute-start | bytes 368648 | tf_op jit(solution)/shard_map/ppermute | solution.py:276
  12.6 40.1 %collective-permute-start.5 = (f32[7,8,1024]{2,1,0:T(8,128)S(1)}, f32[7,8,1024]{2,1,0:T(8,128)S(1)}, u32[]{:S(2)}, u32[]{:S(2)}) collective-permute-start(f32[7,8,1024]{2,1,0:T(8,128)S(1)} %collective-permute-done.4), channel_id=1, source_target_pairs={{256,240},{257,241},{258,242},{259,243},{500,244},{501,245},{502,2... | collective-permute-start | bytes 688136 | tf_op jit(solution)/shard_map/ppermute | solution.py:276
  14.0 38.8 %collective-permute-start.7 = (f32[7,8,1024]{2,1,0:T(8,128)S(1)}, f32[7,8,1024]{2,1,0:T(8,128)S(1)}, u32[]{:S(2)}, u32[]{:S(2)}) collective-permute-start(f32[7,8,1024]{2,1,0:T(8,128)S(1)} %collective-permute-done.6), channel_id=1, source_target_pairs={{304,240},{305,241},{306,242},{307,243},{276,244},{277,245},{278,2... | collective-permute-start | bytes 688136 | tf_op jit(solution)/shard_map/ppermute | solution.py:276
  15.3 37.5 %collective-permute-start.9 = (f32[6,8,1024]{2,1,0:T(8,128)S(1)}, f32[6,8,1024]{2,1,0:T(8,128)S(1)}, u32[]{:S(2)}, u32[]{:S(2)}) collective-permute-start(f32[6,8,1024]{2,1,0:T(8,128)S(1)} %collective-permute-done.8), channel_id=1, source_target_pairs={{448,240},{449,241},{450,242},{451,243},{324,244},{325,245},{326,2... | collective-permute-start | bytes 589832 | tf_op jit(solution)/shard_map/ppermute | solution.py:276
  16.6 7.6 %copy-start.1 = (f32[6,5,8,128]{3,2,1,0:T(8,128)}, f32[6,5,8,128]{3,2,1,0:T(8,128)S(1)}, u32[]{:S(2)}) copy-start(f32[6,5,8,128]{3,2,1,0:T(8,128)S(1)} %collective-permute-done.right) | copy-start | bytes 368644
  16.6 7.6 %collective-permute-start.1 = (f32[6,5,8,128]{3,2,1,0:T(8,128)}, f32[6,5,8,128]{3,2,1,0:T(8,128)S(1)}, u32[]{:S(2)}, u32[]{:S(2)}) collective-permute-start(f32[6,5,8,128]{3,2,1,0:T(8,128)} %get-tuple-element.18), channel_id=1, source_target_pairs={{0,1},{1,2},{2,3},{3,4},{4,5},{5,6},{6,7},{7,8},{8,9},{9,10},{10,1... | collective-permute-start | bytes 368648 | tf_op jit(solution)/shard_map/ppermute | solution.py:276
  24.2 0.7 %copy-start.2 = (f32[6,5,8,128]{3,2,1,0:T(8,128)}, f32[6,5,8,128]{3,2,1,0:T(8,128)S(1)}, u32[]{:S(2)}) copy-start(f32[6,5,8,128]{3,2,1,0:T(8,128)S(1)} %collective-permute-done.1.left) | copy-start | bytes 368644
  31.4 21.4 %collective-permute-start.3 = (f32[5,8,128]{2,1,0:T(8,128)}, f32[5,8,128]{2,1,0:T(8,128)S(1)}, u32[]{:S(2)}, u32[]{:S(2)}) collective-permute-start(f32[5,8,128]{2,1,0:T(8,128)} %get-tuple-element.20), channel_id=1, source_target_pairs={{16,0},{17,1},{18,2},{19,3},{20,4},{21,5},{22,6},{23,7},{24,8},{25... | collective-permute-start | bytes 61448 | tf_op jit(solution)/shard_map/ppermute | solution.py:276
  52.8 0.6 %copy-start.6 = (f32[5,8,128]{2,1,0:T(8,128)}, f32[5,8,128]{2,1,0:T(8,128)S(1)}, u32[]{:S(2)}) copy-start(f32[5,8,128]{2,1,0:T(8,128)S(1)} %collective-permute-done.3.packed) | copy-start | bytes 61444
  52.8 0.7 %copy-start.5 = (f32[6,8,1024]{2,1,0:T(8,128)}, f32[6,8,1024]{2,1,0:T(8,128)S(1)}, u32[]{:S(2)}) copy-start(f32[6,8,1024]{2,1,0:T(8,128)S(1)} %collective-permute-done.9.refs_2_) | copy-start | bytes 589828
  52.8 0.8 %copy-start.3 = (f32[7,8,1024]{2,1,0:T(8,128)}, f32[7,8,1024]{2,1,0:T(8,128)S(1)}, u32[]{:S(2)}) copy-start(f32[7,8,1024]{2,1,0:T(8,128)S(1)} %collective-permute-done.5.refs_0_) | copy-start | bytes 688132
  52.8 0.8 %copy-start.4 = (f32[7,8,1024]{2,1,0:T(8,128)}, f32[7,8,1024]{2,1,0:T(8,128)S(1)}, u32[]{:S(2)}) copy-start(f32[7,8,1024]{2,1,0:T(8,128)S(1)} %collective-permute-done.7.refs_1_) | copy-start | bytes 688132
  52.8 1.0 %copy-start = (f32[4,5,8,1024]{3,2,1,0:T(8,128)}, f32[4,5,8,1024]{3,2,1,0:T(8,128)S(1)}, u32[]{:S(2)}) copy-start(f32[4,5,8,1024]{3,2,1,0:T(8,128)S(1)} %collective-permute-done.2.received) | copy-start | bytes 1966084

commit v2 on v1

--- a/solution.py
+++ b/solution.py
@@ -17,6 +17,8 @@
 WIDE = COLS + LANES
 AXES = ("date", "col")
 
+SLOT = LANES // LAG
+
 PIECES = (7, 7, 6)
 COLUMN_SETS = (
     ((0, 0), (3, 0), (0, 3)),
@@ -55,27 +57,33 @@
     own_low, own_high, edge_low, edge_high = refs[:4]
     pieces = refs[4 : 4 + len(PIECES)]
     buf, sems = refs[4 + len(PIECES) :]
-
-    def copy(j):
-        return pltpu.make_async_copy(
-            slc.at[:, :, :, pl.ds(j * LANES, LANES)], buf.at[j], sems.at[j]
-        )
-
-    for j in range(CHUNKS):
-        copy(j).start()
-    row = AZ * lax.broadcasted_iota(jnp.int32, (LOOKS, LANES), 0)
+    rows = 2 * CHUNKS
+    per_date = AZ * LOOKS * rows
+
+    def copy(d):
+        here = pl.ds(d * per_date, per_date)
+        return pltpu.make_async_copy(slc.at[here], buf.at[here], sems.at[d])
+
+    for d in range(DATES):
+        copy(d).start()
+    look_row = AZ * (lax.broadcasted_iota(jnp.int32, (8, LANES), 0) % LOOKS)
+    lane = lax.broadcasted_iota(jnp.int32, (8, LANES), 1)
     starts = [sum(PIECES[:n]) for n in range(len(PIECES))]
-    for j in range(CHUNKS):
-        copy(j).wait()
-        lanes = slice(j * LANES, (j + 1) * LANES)
-        for d in range(DATES):
-            for q in range(AZ):
-                keep = (row + q >= first[d]) & (row + q < stop[d])
-                tile = []
-                for part in range(2):
-                    value = buf[j, d, part, pl.ds(q, LOOKS, stride=AZ), :]
-                    tile.append(jnp.where(keep, value, 0.0))
-                tile = jnp.concatenate(tile, axis=0)
+    for d in range(DATES):
+        copy(d).wait()
+        for q in range(AZ):
+            keep = (look_row + q >= first[d]) & (look_row + q < stop[d])
+            for j in range(CHUNKS):
+                lanes = slice(j * LANES, (j + 1) * LANES)
+                base = d * per_date + q * rows + 2 * j
+                tile = jnp.concatenate(
+                    [
+                        buf[pl.ds(base + part, LOOKS, stride=AZ * rows), :]
+                        for part in range(2)
+                    ],
+                    axis=0,
+                )
+                tile = jnp.where(keep, tile, 0.0)
                 if d < LAG:
                     own_low[d, q, :, lanes] = tile
                     unit = d * AZ + q
@@ -84,10 +92,16 @@
                             piece[unit - start, :, lanes] = tile
                 else:
                     own_high[d - LAG, q, :, lanes] = tile
-                if j == 0:
-                    edge_low[d, q] = tile
-                if j == CHUNKS - 1:
-                    edge_high[d, q] = tile
+                for edge, at, begin in (
+                    (edge_low, 0, 0),
+                    (edge_high, CHUNKS - 1, -SLOT // 2),
+                ):
+                    if j == at:
+                        slot = d % LAG
+                        here = (lane - SLOT * slot - begin) % LANES < SLOT // 2
+                        moved = lane_roll(tile, SLOT * slot)
+                        rest = 0.0 if slot == 0 else edge[d // LAG, q]
+                        edge[d // LAG, q] = jnp.where(here, moved, rest)
 
 
 def products(a, b, b_swapped):
@@ -120,9 +134,11 @@
     store(2, magnitude[:LOOKS])
 
 
-def inner(own_low, own_high, right, left, used, out, power, packed, sums, powers):
-    lane = lax.broadcasted_iota(jnp.int32, (8, LANES), 1)
-
+def halo_of(edges, d):
+    return [lane_roll(edges[d // LAG, q], -SLOT * (d % LAG)) for q in range(AZ)]
+
+
+def inner(own_low, own_high, edges, used, out, power, sums, powers):
     def chunk(tiles, lanes):
         swapped = [None] + [[half_swap(t) for t in tiles[d]] for d in range(1, DATES)]
         for d in range(DATES):
@@ -131,16 +147,7 @@
             j = i + k + 1
             sums[n, :, lanes] = products(tiles[i], tiles[j], swapped[j])
 
-    halo = [
-        [jnp.where(lane < LANES // 2, right[d, q], left[d, q]) for q in range(AZ)]
-        for d in range(DATES)
-    ]
-    for q in range(AZ):
-        merged = halo[0][q]
-        for d in range(1, LAG):
-            here = (lane >= 32 * d - 16) & (lane < 32 * d + 16)
-            merged = jnp.where(here, lane_roll(halo[d][q], 32 * d), merged)
-        packed[q] = merged
+    halo = [halo_of(edges, d) for d in range(DATES)]
     chunk(halo, pl.ds(COLS, LANES))
 
     @pl.loop(0, CHUNKS)
@@ -168,11 +175,10 @@
         )
 
 
-def outer(own_low, own_high, right, left, power, used, received, packed, *refs):
+def outer(own_low, own_high, edges, power, used, received, their_edges, *refs):
     count = len(PIECES)
     pieces = refs[:count]
     out, sums, powers, staged, sems = refs[count + 1 :]
-    lane = lax.broadcasted_iota(jnp.int32, (8, LANES), 1)
     starts = [sum(PIECES[:n]) for n in range(count)]
     firsts = sorted({i for i, _ in OUTER_PAIRS})
 
@@ -185,11 +191,8 @@
             sums[n, :, lanes] = products(mine[i], theirs[j], swapped[j])
 
     chunk(
-        {
-            d: [jnp.where(lane < LANES // 2, right[d, q], left[d, q]) for q in range(AZ)]
-            for d in firsts
-        },
-        [[lane_roll(packed[q], -32 * d) for q in range(AZ)] for d in range(LAG)],
+        {d: halo_of(edges, d) for d in firsts},
+        [halo_of(their_edges, d) for d in range(LAG)],
         pl.ds(COLS, LANES),
     )
 
@@ -254,23 +257,25 @@
 
 def on_device(slc, first_row, stop_row, pair_used):
     rest = DATES - LAG
+    flat = slc.reshape(DATES, 2, AZ * LOOKS, CHUNKS, LANES).transpose(0, 2, 3, 1, 4)
+    flat = flat.reshape(DATES * AZ * LOOKS * CHUNKS * 2, LANES)
     own_low, own_high, edge_low, edge_high, *pieces = pl.pallas_call(
         prepare,
         out_shape=[
             f32(LAG, AZ, 8, COLS),
             f32(rest, AZ, 8, COLS),
-            f32(DATES, AZ, 8, LANES),
-            f32(DATES, AZ, 8, LANES),
+            f32(2, AZ, 8, LANES),
+            f32(2, AZ, 8, LANES),
         ]
         + [f32(size, 8, COLS) for size in PIECES],
         in_specs=[ANY, SMEM, SMEM],
         out_specs=[VMEM] * (4 + len(PIECES)),
         scratch_shapes=[
-            pltpu.VMEM((CHUNKS, DATES, 2, AZ * LOOKS, LANES), jnp.float32),
-            pltpu.SemaphoreType.DMA((CHUNKS,)),
+            pltpu.VMEM(flat.shape, jnp.float32),
+            pltpu.SemaphoreType.DMA((DATES,)),
         ],
         name="prepare",
-    )(slc, first_row, stop_row)
+    )(flat, first_row, stop_row)
 
     def permute(value, pairs):
         return lax.ppermute(value, AXES, pairs)
@@ -286,28 +291,29 @@
     received = permute(own_low, near)
     left = permute(edge_high, to_right)
     right = permute(edge_low, to_left)
+    edges = right + left
+    their_edges = permute(edges[:1], near + far)
     gathered = [permute(piece, pairs) for piece, pairs in zip(scattered, gather)]
 
     out_shape = f32(DATES, LAG, 3, LOOKS, COLS)
-    out, power, packed = pl.pallas_call(
+    out, power = pl.pallas_call(
         inner,
-        out_shape=[out_shape, f32(DATES, 8, COLS), f32(AZ, 8, LANES)],
-        in_specs=[VMEM] * 4 + [SMEM],
-        out_specs=[VMEM] * 3,
+        out_shape=[out_shape, f32(DATES, 8, COLS)],
+        in_specs=[VMEM] * 3 + [SMEM],
+        out_specs=[VMEM] * 2,
         scratch_shapes=[
             pltpu.VMEM((len(INNER_PAIRS), 8, WIDE), jnp.float32),
             pltpu.VMEM((DATES, 8, WIDE), jnp.float32),
         ],
         name="inner",
-    )(own_low, own_high, right, left, pair_used)
-    their_packed = permute(packed, near + far)
+    )(own_low, own_high, edges, pair_used)
     count = len(PIECES)
     return pl.pallas_call(
         outer,
         out_shape=out_shape,
-        in_specs=[VMEM] * 5 + [SMEM] + [VMEM] * (2 + count) + [ANY],
+        in_specs=[VMEM] * 4 + [SMEM] + [VMEM] * (2 + count) + [ANY],
         out_specs=ANY,
-        input_output_aliases={8 + count: 0},
+        input_output_aliases={7 + count: 0},
         scratch_shapes=[
             pltpu.VMEM((len(OUTER_PAIRS), 8, WIDE), jnp.float32),
             pltpu.VMEM((LAG, 8, WIDE), jnp.float32),
@@ -315,7 +321,17 @@
             pltpu.SemaphoreType.DMA((len(OUTER_PAIRS),)),
         ],
         name="outer",
-    )(own_low, own_high, right, left, power, pair_used, received, their_packed, *gathered, out)
+    )(
+        own_low,
+        own_high,
+        edges,
+        power,
+        pair_used,
+        received,
+        their_edges,
+        *gathered,
+        out,
+    )
 
 
 def solution(mesh):

time: 59.5 us -> 52.6 us (0.88)
  waiting for transfers between devices: 23.7 us -> 18.2 us
  local copies, waits for them, and re-layouts: 4.91 us -> 2.41 us
  starting transfers between devices: 15.2 us -> 16.3 us
    ppermute x10, waiting for transfers between devices: 23.7 us -> 18.2 us  [permute(): return lax.ppermute(value, AXES, pairs)]
    unnamed x18 -> x13, local copies, waits for them, and re-layouts: 4.91 us -> 2.4 us
    ppermute x10, starting transfers between devices: 15.2 us -> 16.3 us  [permute(): return lax.ppermute(value, AXES, pairs)]
  transfers between devices with their start and end apart: 10 -> 10, of which waited for: 2 -> 3; matrix products, arithmetic and copies ran while one was open for 1% -> 3% of each run, Pallas kernels for 11% -> 12%
where the time goes in v2:
time: 52.6 us; the launch traced here: 52.2 us
  waiting for transfers between devices  18.2 us (35%)
  starting transfers between devices  16.3 us (31%)
  Pallas kernels  15.1 us (29%)
  local copies, waits for them, and re-layouts  2.41 us (5%)
    ppermute x10, waiting for transfers between devices, permute(): return lax.ppermute(value, AXES, pairs)  18.2 us
    ppermute x10, starting transfers between devices, permute(): return lax.ppermute(value, AXES, pairs)  16.3 us
    pallas_call x1, Pallas kernels, on_device(): pl.pallas_call(inner, out_shape=[out_shape, f32(DATES, 8, COLS)], in_spec...  6.52 us
    pallas_call x1, Pallas kernels, on_device(): pl.pallas_call(outer, out_shape=out_shape, in_specs=[VMEM] * 4 + [SMEM] +...  5.22 us
    pallas_call x1, Pallas kernels, on_device(): pl.pallas_call(prepare, out_shape=[f32(LAG, AZ, 8, COLS), f32(rest, AZ, 8...  3.38 us
    unnamed x13, local copies, waits for them, and re-layouts  2.4 us
  transfers between devices with their start and end apart: 10, of which 3 were waited for; matrix products, arithmetic and copies ran while one was open for 3% of the time, Pallas kernels for 12%

profile of v2, /device:TPU:158, one launch (start us, length us, event | category | flops | bytes accessed | tf_op | source)
XLA Modules:
  0.0 52.2 jit_solution(1611479957762644582)
XLA Ops:
  0.0 3.4 %prepare.1 = (f32[4,5,8,1024]{3,2,1,0:T(8,128)}, f32[2,5,8,1024]{3,2,1,0:T(8,128)}, f32[2,5,8,128]{3,2,1,0:T(8,128)}, f32[2,5,8,128]{3,2,1,0:T(8,128)}, f32[7,8,...) custom-call(f32[1920,128]{1,0:T(8,128)} %bitcast.5, s32[6]{0:T(128)} %first.1, s32[6]{0:T(128)} %stop.1), custom_call_target="tpu_custom_call" | custom-call | tf_op jit(solution)/shard_map/prepare/pallas_call | solution.py:262
  3.4 2.8 %collective-permute-start.2 = (f32[4,5,8,1024]{3,2,1,0:T(8,128)}, f32[4,5,8,1024]{3,2,1,0:T(8,128)S(1)}, u32[]{:S(2)}, u32[]{:S(2)}) collective-permute-start(f32[4,5,8,1024]{3,2,1,0:T(8,128)} %get-tuple-element.14.own_low), channel_id=1, source_target_pairs={{16,0},{17,1},{18,2},{19,3},{20,4},{21,5},{22,6},{23,7},{24,8},{25... | collective-permute-start | bytes 1966088 | tf_op jit(solution)/shard_map/ppermute | solution.py:281
  6.2 0.7 %collective-permute-start.4 = (f32[7,8,1024]{2,1,0:T(8,128)}, f32[7,8,1024]{2,1,0:T(8,128)S(1)}, u32[]{:S(2)}, u32[]{:S(2)}) collective-permute-start(f32[7,8,1024]{2,1,0:T(8,128)} %get-tuple-element.19), channel_id=1, source_target_pairs={{256,256},{257,257},{258,258},{259,259},{260,500},{261,501},{262,5... | collective-permute-start | bytes 688136 | tf_op jit(solution)/shard_map/ppermute | solution.py:281
  6.9 0.7 %collective-permute-start.6 = (f32[7,8,1024]{2,1,0:T(8,128)}, f32[7,8,1024]{2,1,0:T(8,128)S(1)}, u32[]{:S(2)}, u32[]{:S(2)}) collective-permute-start(f32[7,8,1024]{2,1,0:T(8,128)} %get-tuple-element.20), channel_id=1, source_target_pairs={{256,304},{257,305},{258,306},{259,307},{260,276},{261,277},{262,2... | collective-permute-start | bytes 688136 | tf_op jit(solution)/shard_map/ppermute | solution.py:281
  7.5 0.7 %collective-permute-start.8 = (f32[6,8,1024]{2,1,0:T(8,128)}, f32[6,8,1024]{2,1,0:T(8,128)S(1)}, u32[]{:S(2)}, u32[]{:S(2)}) collective-permute-start(f32[6,8,1024]{2,1,0:T(8,128)} %get-tuple-element.21), channel_id=1, source_target_pairs={{256,448},{257,449},{258,450},{259,451},{260,324},{261,325},{262,3... | collective-permute-start | bytes 589832 | tf_op jit(solution)/shard_map/ppermute | solution.py:281
  8.2 0.0 collective-permute-done.4
  8.2 1.3 %collective-permute-start.5 = (f32[7,8,1024]{2,1,0:T(8,128)S(1)}, f32[7,8,1024]{2,1,0:T(8,128)S(1)}, u32[]{:S(2)}, u32[]{:S(2)}) collective-permute-start(f32[7,8,1024]{2,1,0:T(8,128)S(1)} %collective-permute-done.4), channel_id=1, source_target_pairs={{256,240},{257,241},{258,242},{259,243},{500,244},{501,245},{502,2... | collective-permute-start | bytes 688136 | tf_op jit(solution)/shard_map/ppermute | solution.py:281
  9.5 0.0 collective-permute-done.6
  9.5 1.3 %collective-permute-start.7 = (f32[7,8,1024]{2,1,0:T(8,128)S(1)}, f32[7,8,1024]{2,1,0:T(8,128)S(1)}, u32[]{:S(2)}, u32[]{:S(2)}) collective-permute-start(f32[7,8,1024]{2,1,0:T(8,128)S(1)} %collective-permute-done.6), channel_id=1, source_target_pairs={{304,240},{305,241},{306,242},{307,243},{276,244},{277,245},{278,2... | collective-permute-start | bytes 688136 | tf_op jit(solution)/shard_map/ppermute | solution.py:281
  10.8 0.0 collective-permute-done.8
  10.8 1.3 %collective-permute-start.9 = (f32[6,8,1024]{2,1,0:T(8,128)S(1)}, f32[6,8,1024]{2,1,0:T(8,128)S(1)}, u32[]{:S(2)}, u32[]{:S(2)}) collective-permute-start(f32[6,8,1024]{2,1,0:T(8,128)S(1)} %collective-permute-done.8), channel_id=1, source_target_pairs={{448,240},{449,241},{450,242},{451,243},{324,244},{325,245},{326,2... | collective-permute-start | bytes 589832 | tf_op jit(solution)/shard_map/ppermute | solution.py:281
  12.1 1.9 %collective-permute-start = (f32[2,5,8,128]{3,2,1,0:T(8,128)}, f32[2,5,8,128]{3,2,1,0:T(8,128)S(1)}, u32[]{:S(2)}, u32[]{:S(2)}) collective-permute-start(f32[2,5,8,128]{3,2,1,0:T(8,128)} %get-tuple-element.16), channel_id=1, source_target_pairs={{1,0},{2,1},{3,2},{4,3},{5,4},{6,5},{7,6},{8,7},{9,8},{10,9},{11,1... | collective-permute-start | bytes 122888 | tf_op jit(solution)/shard_map/ppermute | solution.py:281
  14.1 2.0 %collective-permute-done = f32[2,5,8,128]{3,2,1,0:T(8,128)S(1)} collective-permute-done((f32[2,5,8,128]{3,2,1,0:T(8,128)}, f32[2,5,8,128]{3,2,1,0:T(8,128)S(1)}, u32[]{:S(2)}, u32[]{:S(2)}) %collective-permute-start) | collective-permute-done | bytes 40992 | tf_op jit(solution)/shard_map/ppermute | solution.py:281
  16.0 3.8 %collective-permute-start.1 = (f32[2,5,8,128]{3,2,1,0:T(8,128)}, f32[2,5,8,128]{3,2,1,0:T(8,128)S(1)}, u32[]{:S(2)}, u32[]{:S(2)}) collective-permute-start(f32[2,5,8,128]{3,2,1,0:T(8,128)} %get-tuple-element.17), channel_id=1, source_target_pairs={{0,1},{1,2},{2,3},{3,4},{4,5},{5,6},{6,7},{7,8},{8,9},{9,10},{10,1... | collective-permute-start | bytes 122888 | tf_op jit(solution)/shard_map/ppermute | solution.py:281
  19.9 2.9 %collective-permute-done.1 = f32[2,5,8,128]{3,2,1,0:T(8,128)S(1)} collective-permute-done((f32[2,5,8,128]{3,2,1,0:T(8,128)}, f32[2,5,8,128]{3,2,1,0:T(8,128)S(1)}, u32[]{:S(2)}, u32[]{:S(2)}) %collective-permute-start.1) | collective-permute-done | bytes 40992 | tf_op jit(solution)/shard_map/ppermute | solution.py:281
  22.8 1.9 %collective-permute-start.3 = (f32[1,5,8,128]{3,2,1,0:T(8,128)S(1)}, f32[1,5,8,128]{3,2,1,0:T(8,128)S(1)}, u32[]{:S(2)}, u32[]{:S(2)}) collective-permute-start(f32[1,5,8,128]{3,2,1,0:T(8,128)S(1)} %slice.4), channel_id=1, source_target_pairs={{16,0},{17,1},{18,2},{19,3},{20,4},{21,5},{22,6},{23,7},{24,8},{25... | collective-permute-start | bytes 61448 | tf_op jit(solution)/shard_map/ppermute | solution.py:281
  24.7 1.4 %copy.7.used = s32[6,4]{1,0:T(8,128)} copy(s32[6,4]{0,1:T(4,128)} %param.7) | data formatting | bytes 192 | tf_op args[3]
  26.1 0.0 copy-done.1
  26.1 6.5 %inner.1 = (f32[6,4,3,4,1024]{4,3,2,1,0:T(4,128)}, f32[6,8,1024]{2,1,0:T(8,128)}) custom-call(f32[4,5,8,1024]{3,2,1,0:T(8,128)} %get-tuple-element.14.own_low, f32[2,5,8,1024]{3,2,1,0:T(8,128)} %get-tuple-element.15.own_high, f32[2,5,8,128]{3,2,1,0:T(8,128)} %copy-done.1, s32[6,4]{1,0:T(8,128)} %copy.7.used), custom_call_target="tpu_custom_call" | custom-call | tf_op jit(solution)/shard_map/inner/pallas_call | solution.py:299
  32.6 13.3 %collective-permute-done.3.their_edges = f32[1,5,8,128]{3,2,1,0:T(8,128)S(1)} collective-permute-done((f32[1,5,8,128]{3,2,1,0:T(8,128)S(1)}, f32[1,5,8,128]{3,2,1,0:T(8,128)S(1)}, u32[]{:S(2)}, u32[]{:S(2)}) %collective-permute-start.3) | collective-permute-done | bytes 20512 | tf_op jit(solution)/shard_map/ppermute | solution.py:281
  45.9 0.0 collective-permute-done.9.refs_2_
  45.9 0.0 collective-permute-done.5.refs_0_
  45.9 0.0 copy-start.2
  45.9 0.0 collective-permute-done.7.refs_1_
  45.9 0.0 copy-start.3
  45.9 0.0 collective-permute-done.2.received
  45.9 0.5 %copy-done.5 = f32[1,5,8,128]{3,2,1,0:T(8,128)} copy-done((f32[1,5,8,128]{3,2,1,0:T(8,128)}, f32[1,5,8,128]{3,2,1,0:T(8,128)S(1)}, u32[]{:S(2)}) %copy-start.5) | copy-done | bytes 20504
  46.5 0.1 copy-done.4
  46.6 0.1 copy-done.2
  46.6 0.1 copy-done.3
  46.7 0.2 copy-done
  47.0 5.2 %outer.1 = f32[6,4,3,4,1024]{4,3,2,1,0:T(4,128)} custom-call(f32[4,5,8,1024]{3,2,1,0:T(8,128)} %get-tuple-element.14.own_low, f32[2,5,8,1024]{3,2,1,0:T(8,128)} %get-tuple-element.15.own_high, f32[2,5,8,128]{3,2,1,0:T(8,128)} %copy-done.1, f32[6,8,1024]{2,1,0:T(8,128)} %get-tuple-element.18.power, ...), custom_call_target="tpu_custom_call", output_to_operand_aliasing={{}: (10, {})} | custom-call | tf_op jit(solution)/shard_map/outer/pallas_call | solution.py:311
  (6 shorter events, 0.0 us)
Async XLA Ops:
  3.4 42.5 %collective-permute-start.2 = (f32[4,5,8,1024]{3,2,1,0:T(8,128)}, f32[4,5,8,1024]{3,2,1,0:T(8,128)S(1)}, u32[]{:S(2)}, u32[]{:S(2)}) collective-permute-start(f32[4,5,8,1024]{3,2,1,0:T(8,128)} %get-tuple-element.14.own_low), channel_id=1, source_target_pairs={{16,0},{17,1},{18,2},{19,3},{20,4},{21,5},{22,6},{23,7},{24,8},{25... | collective-permute-start | bytes 1966088 | tf_op jit(solution)/shard_map/ppermute | solution.py:281
  6.2 2.0 %collective-permute-start.4 = (f32[7,8,1024]{2,1,0:T(8,128)}, f32[7,8,1024]{2,1,0:T(8,128)S(1)}, u32[]{:S(2)}, u32[]{:S(2)}) collective-permute-start(f32[7,8,1024]{2,1,0:T(8,128)} %get-tuple-element.19), channel_id=1, source_target_pairs={{256,256},{257,257},{258,258},{259,259},{260,500},{261,501},{262,5... | collective-permute-start | bytes 688136 | tf_op jit(solution)/shard_map/ppermute | solution.py:281
  6.9 2.7 %collective-permute-start.6 = (f32[7,8,1024]{2,1,0:T(8,128)}, f32[7,8,1024]{2,1,0:T(8,128)S(1)}, u32[]{:S(2)}, u32[]{:S(2)}) collective-permute-start(f32[7,8,1024]{2,1,0:T(8,128)} %get-tuple-element.20), channel_id=1, source_target_pairs={{256,304},{257,305},{258,306},{259,307},{260,276},{261,277},{262,2... | collective-permute-start | bytes 688136 | tf_op jit(solution)/shard_map/ppermute | solution.py:281
  7.5 3.3 %collective-permute-start.8 = (f32[6,8,1024]{2,1,0:T(8,128)}, f32[6,8,1024]{2,1,0:T(8,128)S(1)}, u32[]{:S(2)}, u32[]{:S(2)}) collective-permute-start(f32[6,8,1024]{2,1,0:T(8,128)} %get-tuple-element.21), channel_id=1, source_target_pairs={{256,448},{257,449},{258,450},{259,451},{260,324},{261,325},{262,3... | collective-permute-start | bytes 589832 | tf_op jit(solution)/shard_map/ppermute | solution.py:281
  8.2 37.7 %collective-permute-start.5 = (f32[7,8,1024]{2,1,0:T(8,128)S(1)}, f32[7,8,1024]{2,1,0:T(8,128)S(1)}, u32[]{:S(2)}, u32[]{:S(2)}) collective-permute-start(f32[7,8,1024]{2,1,0:T(8,128)S(1)} %collective-permute-done.4), channel_id=1, source_target_pairs={{256,240},{257,241},{258,242},{259,243},{500,244},{501,245},{502,2... | collective-permute-start | bytes 688136 | tf_op jit(solution)/shard_map/ppermute | solution.py:281
  9.5 36.4 %collective-permute-start.7 = (f32[7,8,1024]{2,1,0:T(8,128)S(1)}, f32[7,8,1024]{2,1,0:T(8,128)S(1)}, u32[]{:S(2)}, u32[]{:S(2)}) collective-permute-start(f32[7,8,1024]{2,1,0:T(8,128)S(1)} %collective-permute-done.6), channel_id=1, source_target_pairs={{304,240},{305,241},{306,242},{307,243},{276,244},{277,245},{278,2... | collective-permute-start | bytes 688136 | tf_op jit(solution)/shard_map/ppermute | solution.py:281
  10.8 35.0 %collective-permute-start.9 = (f32[6,8,1024]{2,1,0:T(8,128)S(1)}, f32[6,8,1024]{2,1,0:T(8,128)S(1)}, u32[]{:S(2)}, u32[]{:S(2)}) collective-permute-start(f32[6,8,1024]{2,1,0:T(8,128)S(1)} %collective-permute-done.8), channel_id=1, source_target_pairs={{448,240},{449,241},{450,242},{451,243},{324,244},{325,245},{326,2... | collective-permute-start | bytes 589832 | tf_op jit(solution)/shard_map/ppermute | solution.py:281
  12.1 3.9 %collective-permute-start = (f32[2,5,8,128]{3,2,1,0:T(8,128)}, f32[2,5,8,128]{3,2,1,0:T(8,128)S(1)}, u32[]{:S(2)}, u32[]{:S(2)}) collective-permute-start(f32[2,5,8,128]{3,2,1,0:T(8,128)} %get-tuple-element.16), channel_id=1, source_target_pairs={{1,0},{2,1},{3,2},{4,3},{5,4},{6,5},{7,6},{8,7},{9,8},{10,9},{11,1... | collective-permute-start | bytes 122888 | tf_op jit(solution)/shard_map/ppermute | solution.py:281
  16.0 6.7 %collective-permute-start.1 = (f32[2,5,8,128]{3,2,1,0:T(8,128)}, f32[2,5,8,128]{3,2,1,0:T(8,128)S(1)}, u32[]{:S(2)}, u32[]{:S(2)}) collective-permute-start(f32[2,5,8,128]{3,2,1,0:T(8,128)} %get-tuple-element.17), channel_id=1, source_target_pairs={{0,1},{1,2},{2,3},{3,4},{4,5},{5,6},{6,7},{7,8},{8,9},{9,10},{10,1... | collective-permute-start | bytes 122888 | tf_op jit(solution)/shard_map/ppermute | solution.py:281
  22.8 3.3 %copy-start.1 = (f32[2,5,8,128]{3,2,1,0:T(8,128)}, f32[2,5,8,128]{3,2,1,0:T(8,128)S(1)}, u32[]{:S(2)}) copy-start(f32[2,5,8,128]{3,2,1,0:T(8,128)S(1)} %add.3.edges) | copy-start | bytes 122884
  22.8 23.1 %collective-permute-start.3 = (f32[1,5,8,128]{3,2,1,0:T(8,128)S(1)}, f32[1,5,8,128]{3,2,1,0:T(8,128)S(1)}, u32[]{:S(2)}, u32[]{:S(2)}) collective-permute-start(f32[1,5,8,128]{3,2,1,0:T(8,128)S(1)} %slice.4), channel_id=1, source_target_pairs={{16,0},{17,1},{18,2},{19,3},{20,4},{21,5},{22,6},{23,7},{24,8},{25... | collective-permute-start | bytes 61448 | tf_op jit(solution)/shard_map/ppermute | solution.py:281
  45.9 0.6 %copy-start.5 = (f32[1,5,8,128]{3,2,1,0:T(8,128)}, f32[1,5,8,128]{3,2,1,0:T(8,128)S(1)}, u32[]{:S(2)}) copy-start(f32[1,5,8,128]{3,2,1,0:T(8,128)S(1)} %collective-permute-done.3.their_edges) | copy-start | bytes 61444
  45.9 0.7 %copy-start.4 = (f32[6,8,1024]{2,1,0:T(8,128)}, f32[6,8,1024]{2,1,0:T(8,128)S(1)}, u32[]{:S(2)}) copy-start(f32[6,8,1024]{2,1,0:T(8,128)S(1)} %collective-permute-done.9.refs_2_) | copy-start | bytes 589828
  45.9 0.8 %copy-start.2 = (f32[7,8,1024]{2,1,0:T(8,128)}, f32[7,8,1024]{2,1,0:T(8,128)S(1)}, u32[]{:S(2)}) copy-start(f32[7,8,1024]{2,1,0:T(8,128)S(1)} %collective-permute-done.5.refs_0_) | copy-start | bytes 688132
  45.9 0.8 %copy-start.3 = (f32[7,8,1024]{2,1,0:T(8,128)}, f32[7,8,1024]{2,1,0:T(8,128)S(1)}, u32[]{:S(2)}) copy-start(f32[7,8,1024]{2,1,0:T(8,128)S(1)} %collective-permute-done.7.refs_1_) | copy-start | bytes 688132
  45.9 1.0 %copy-start = (f32[4,5,8,1024]{3,2,1,0:T(8,128)}, f32[4,5,8,1024]{3,2,1,0:T(8,128)S(1)}, u32[]{:S(2)}) copy-start(f32[4,5,8,1024]{3,2,1,0:T(8,128)S(1)} %collective-permute-done.2.received) | copy-start | bytes 1966084

commit v3 on v0

v3 whole, which is shorter than its diff:
```python
import jax
import jax.numpy as jnp
from jax import lax
from jax.experimental import pallas as pl
from jax.experimental.pallas import tpu as pltpu
from jax.sharding import PartitionSpec as P

AZ = 5
LAG = 4
DATES = 6
LOOKS = 4
COLS = 1024
MARGIN = 10
LANES = 128
CHUNKS = COLS // LANES
GROUP = 2 * LANES
ROW = 2 * CHUNKS
PER_DATE = AZ * LOOKS * ROW
WIDE = COLS + 2 * LANES
AXES = ("date", "col")

SLOT = LANES // LAG

PIECES = (10, 10)
COUNT = len(PIECES)
STARTS = [sum(PIECES[:n]) for n in range(COUNT)]
COLUMN_SETS = (
    (((0, 0), (3, 0)), ((0, 3), (3, 3))),
    (((1, 0), (0, 1)), ((2, 3), (3, 2))),
    (((2, 0), (0, 2)), ((1, 3), (3, 1))),
    (((1, 1), (2, 2)), ((2, 1), (1, 2))),
)
SOURCE_XY = (0, 0)
TARGET_XY = (3, 3)

INNER_PAIRS = [(i, k) for i in range(DATES) for k in range(LAG) if i + k + 1 < DATES]
OUTER_PAIRS = [(i, k) for i in range(DATES) for k in range(LAG) if i + k + 1 >= DATES]
OUTER_FIRST = min(i for i, _ in OUTER_PAIRS)

VMEM = pl.BlockSpec(memory_space=pltpu.VMEM)
SMEM = pl.BlockSpec(memory_space=pltpu.SMEM)
ANY = pl.BlockSpec(memory_space=pl.ANY)
PARAMS = pltpu.CompilerParams(vmem_limit_bytes=16 * 1024 * 1024)


def f32(*shape):
    return jax.ShapeDtypeStruct(shape, jnp.float32)


def lane_roll(x, by):
    return pltpu.roll(x, by % x.shape[-1], axis=x.ndim - 1)


def half_swap(x):
    return pltpu.roll(x, LOOKS, axis=0)


def upper(x):
    return lax.broadcasted_iota(jnp.int32, x.shape, 0) < LOOKS


def place(unit):
    n = max(n for n in range(COUNT) if STARTS[n] <= unit)
    return n, unit - STARTS[n]


def masked_tile(buf, first, stop, d, q, j, base):
    row = AZ * (lax.broadcasted_iota(jnp.int32, (8, LANES), 0) % LOOKS) + q
    keep = (row >= first[d]) & (row < stop[d])
    at = base + q * ROW + 2 * j
    tile = jnp.concatenate(
        [buf[pl.ds(at + part, LOOKS, stride=AZ * ROW), :] for part in range(2)], axis=0
    )
    return jnp.where(keep, tile, 0.0)


def load_dates(slc, buf, sems, dates):
    copies = [
        pltpu.make_async_copy(
            slc.at[pl.ds(d * PER_DATE, PER_DATE)],
            buf.at[pl.ds(n * PER_DATE, PER_DATE)],
            sems.at[n],
        )
        for n, d in enumerate(dates)
    ]
    for copy in copies:
        copy.start()
    return copies


def prepare(slc, first, stop, *refs):
    pieces = refs[:COUNT]
    low, edge_low, edge_high, buf, sems = refs[COUNT:]
    copies = load_dates(slc, buf, sems, range(DATES))
    lane = lax.broadcasted_iota(jnp.int32, (8, LANES), 1)
    for d in range(DATES):
        copies[d].wait()
        slot = d % LAG
        for q in range(AZ):
            for j in range(CHUNKS):
                is_edge = j in (0, CHUNKS - 1)
                if d >= LAG and not is_edge:
                    continue
                tile = masked_tile(buf, first, stop, d, q, j, d * PER_DATE)
                if d < LAG:
                    n, at = place(d * AZ + q)
                    lanes = slice(j * LANES, (j + 1) * LANES)
                    pieces[n][at, :, lanes] = tile
                    low[d * AZ + q, :, lanes] = tile
                if is_edge:
                    edge, begin = (edge_low, 0) if j == 0 else (edge_high, -SLOT // 2)
                    here = (lane - SLOT * slot - begin) % LANES < SLOT // 2
                    rest = 0.0 if slot == 0 else edge[d // LAG, q]
                    edge[d // LAG, q] = jnp.where(here, lane_roll(tile, SLOT * slot), rest)


def lay_out_last(slc, first, stop, high, buf, sems):
    copies = load_dates(slc, buf, sems, range(LAG, DATES))
    for d in range(LAG, DATES):
        copies[d - LAG].wait()
        for q in range(AZ):
            for j in range(CHUNKS):
                high[d - LAG, q, :, j * LANES : (j + 1) * LANES] = masked_tile(
                    buf, first, stop, d, q, j, (d - LAG) * PER_DATE
                )


def halo_of(edges, d):
    return [lane_roll(edges[d // LAG, q], -SLOT * (d % LAG)) for q in range(AZ)]


def products(a, b, b_swapped):
    straight = a[0] * b[0]
    crossed = a[0] * b_swapped[0]
    for q in range(1, AZ):
        straight = straight + a[q] * b[q]
        crossed = crossed + a[q] * b_swapped[q]
    return jnp.where(
        upper(straight), straight + half_swap(straight), crossed - half_swap(crossed)
    )


def power_of(a):
    total = a[0] * a[0]
    for q in range(1, AZ):
        total = total + a[q] * a[q]
    return total + half_swap(total)


def look_sums(sums, pairs, shift, mine, theirs, powered, lanes):
    swapped = {j: [half_swap(t) for t in theirs[j]] for j in {i + k + 1 - shift for i, k in pairs}}
    for n, (i, k) in enumerate(pairs):
        j = i + k + 1 - shift
        sums[8 * n : 8 * n + 8, lanes] = products(mine[i], theirs[j], swapped[j])
    for m in range(len(powered) // 2):
        one, two = power_of(powered[2 * m]), power_of(powered[2 * m + 1])
        at = 8 * (len(pairs) + m)
        sums[at : at + 8, lanes] = jnp.where(upper(one), one, two)


def fill(sums, tiles_at, halo, body):
    body(halo, pl.ds(0, LANES))
    rows = sums.shape[0]
    sums[:, COLS + LANES :] = sums[:, :LANES].reshape(rows, LANES)

    @pl.loop(0, CHUNKS)
    def _(c):
        body(
            tiles_at(pl.ds(pl.multiple_of(c * LANES, LANES), LANES)),
            pl.ds(pl.multiple_of((c + 1) * LANES, LANES), LANES),
        )


def windows(sums, g):
    k = lax.broadcasted_iota(jnp.int32, (2 * GROUP, GROUP), 0) - LANES
    n = lax.broadcasted_iota(jnp.int32, (2 * GROUP, GROUP), 1)
    band = ((k >= n - MARGIN) & (k < n + MARGIN)).astype(jnp.float32).astype(jnp.bfloat16)
    left = sums[:, g * GROUP : (g + 2) * GROUP]
    total = None
    for _ in range(3):
        term = left.astype(jnp.bfloat16)
        left = left - term.astype(jnp.float32)
        part = jnp.dot(term, band, preferred_element_type=jnp.float32)
        total = part if total is None else total + part
    return total


def unpacked_powers(result, base, count):
    powers = []
    for m in range(count // 2):
        both = result[base + 8 * m : base + 8 * m + 8]
        other = half_swap(both)
        powers.append(jnp.where(upper(both), both, other))
        powers.append(jnp.where(upper(both), other, both))
    return powers


def write_pair(store, cross, power_first, power_second, used):
    gamma = cross * (used * lax.rsqrt(jnp.maximum(power_first * power_second, 1.0)))
    square = gamma * gamma
    magnitude = jnp.sqrt(square + half_swap(square))
    store(0, gamma[:LOOKS])
    store(1, gamma[LOOKS:])
    store(2, magnitude[:LOOKS])


def own_tiles(pieces, high, lanes, dates):
    tiles = {}
    for d in dates:
        if d < LAG:
            units = [place(d * AZ + q) for q in range(AZ)]
            tiles[d] = [pieces[n][at, :, lanes] for n, at in units]
        else:
            tiles[d] = [high[d - LAG, q, :, lanes] for q in range(AZ)]
    return tiles


def inner(*refs):
    pieces = refs[:COUNT]
    slc, first, stop, edges, used, out, power, high, sums, buf, sems = refs[COUNT:]
    dates = range(DATES)
    lay_out_last(slc, first, stop, high, buf, sems)

    def body(tiles, lanes):
        powered = [tiles[d] for d in dates]
        look_sums(sums, INNER_PAIRS, 0, tiles, tiles, powered, lanes)

    fill(
        sums,
        lambda lanes: own_tiles(pieces, high, lanes, dates),
        {d: halo_of(edges, d) for d in dates},
        body,
    )
    for g in range(COLS // GROUP):
        lanes = slice(g * GROUP, (g + 1) * GROUP)
        result = windows(sums, g)
        powers = unpacked_powers(result, 8 * len(INNER_PAIRS), DATES)
        for d in range(OUTER_FIRST, DATES):
            power[d - OUTER_FIRST, :, lanes] = powers[d]
        for n, (i, k) in enumerate(INNER_PAIRS):

            def store(m, value, i=i, k=k, lanes=lanes):
                out[i, k, m, :, lanes] = value

            write_pair(
                store,
                result[8 * n : 8 * n + 8],
                powers[i],
                powers[i + k + 1],
                used[i, k].astype(jnp.float32),
            )


def outer(*refs):
    pieces = refs[:COUNT]
    high, edges, power, used, received, their_edges = refs[COUNT : COUNT + 6]
    far = refs[COUNT + 6 : 2 * COUNT + 6]
    out, sums, staged, sems = refs[2 * COUNT + 7 :]
    dates = range(OUTER_FIRST, DATES)

    def body(tiles, lanes):
        mine, theirs = tiles
        look_sums(sums, OUTER_PAIRS, DATES, mine, theirs, theirs, lanes)

    def tiles_at(lanes):
        theirs = []
        for d in range(LAG):
            units = [d * AZ + q for q in range(AZ)]
            theirs.append(
                [
                    received[unit, :, lanes] + far[place(unit)[0]][place(unit)[1], :, lanes]
                    for unit in units
                ]
            )
        return own_tiles(pieces, high, lanes, dates), theirs

    fill(
        sums,
        tiles_at,
        (
            {d: halo_of(edges, d) for d in dates},
            [halo_of(their_edges, d) for d in range(LAG)],
        ),
        body,
    )
    for g in range(COLS // GROUP):
        lanes = slice(g * GROUP, (g + 1) * GROUP)
        result = windows(sums, g)
        powers = unpacked_powers(result, 8 * len(OUTER_PAIRS), LAG)
        for n, (i, k) in enumerate(OUTER_PAIRS):

            def store(m, value, n=n, lanes=lanes):
                staged[n, m, :, lanes] = value

            write_pair(
                store,
                result[8 * n : 8 * n + 8],
                power[i - OUTER_FIRST, :, lanes],
                powers[i + k + 1 - DATES],
                used[i, k].astype(jnp.float32),
            )
    copies = [
        pltpu.make_async_copy(staged.at[n], out.at[i, k], sems.at[n])
        for n, (i, k) in enumerate(OUTER_PAIRS)
    ]
    for copy in copies:
        copy.start()
    for copy in copies:
        copy.wait()


def far_permutes():
    def flat(x, y, z, core):
        return ((z // 8) * 16 + y * 4 + x) * 16 + (z % 8) * 2 + core

    scatter = [[] for _ in PIECES]
    gather = [[] for _ in PIECES]
    for z in range(8):
        for core in range(2):
            for n, (x, y) in enumerate(COLUMN_SETS[z // 2][core]):
                relay = flat(x, y, 8 + z, core)
                scatter[n].append((flat(*SOURCE_XY, 8 + z, core), relay))
                gather[n].append((relay, flat(*TARGET_XY, z, core)))
    return scatter, gather


def sum_rows(pairs, dates):
    return 8 * (len(pairs) + dates // 2)


def on_device(slc, first_row, stop_row, pair_used):
    slc = slc.reshape(DATES, 2, AZ * LOOKS, CHUNKS, LANES).transpose(0, 2, 3, 1, 4)
    slc = slc.reshape(DATES * PER_DATE, LANES)
    piece_shapes = [f32(size, 8, COLS) for size in PIECES]
    edge_shape = f32(2, AZ, 8, LANES)
    *pieces, low, edge_low, edge_high = pl.pallas_call(
        prepare,
        out_shape=piece_shapes + [f32(LAG * AZ, 8, COLS), edge_shape, edge_shape],
        in_specs=[ANY, SMEM, SMEM],
        out_specs=[VMEM] * (COUNT + 3),
        scratch_shapes=[
            pltpu.VMEM((DATES * PER_DATE, LANES), jnp.float32),
            pltpu.SemaphoreType.DMA((DATES,)),
        ],
        name="prepare",
    )(slc, first_row, stop_row)

    def permute(value, pairs):
        return lax.ppermute(value, AXES, pairs)

    near = [
        (d * 16 + c, (d - 1) * 16 + c) for d in range(1, 32) if d != 16 for c in range(16)
    ]
    far = [(16 * 16 + c, 15 * 16 + c) for c in range(16)]
    to_right = [(d * 16 + c, d * 16 + c + 1) for d in range(32) for c in range(15)]
    to_left = [(b, a) for a, b in to_right]
    scatter, gather = far_permutes()

    scattered = [permute(piece, pairs) for piece, pairs in zip(pieces, scatter)]
    left = permute(edge_high, to_right)
    right = permute(edge_low, to_left)
    received = permute(low, near)
    edges, *scattered = lax.optimization_barrier((right + left, *scattered))
    gathered = [permute(piece, pairs) for piece, pairs in zip(scattered, gather)]
    their_edges = permute(edges[:1], near + far)

    out_shape = f32(DATES, LAG, 3, LOOKS, COLS)
    out, power, high = pl.pallas_call(
        inner,
        out_shape=[
            out_shape,
            f32(DATES - OUTER_FIRST, 8, COLS),
            f32(DATES - LAG, AZ, 8, COLS),
        ],
        in_specs=[VMEM] * COUNT + [ANY, SMEM, SMEM, VMEM, SMEM],
        out_specs=[VMEM] * 3,
        scratch_shapes=[
            pltpu.VMEM((sum_rows(INNER_PAIRS, DATES), WIDE), jnp.float32),
            pltpu.VMEM(((DATES - LAG) * PER_DATE, LANES), jnp.float32),
            pltpu.SemaphoreType.DMA((DATES - LAG,)),
        ],
        compiler_params=PARAMS,
        name="inner",
    )(*pieces, slc, first_row, stop_row, edges, pair_used)
    return pl.pallas_call(
        outer,
        out_shape=out_shape,
        in_specs=[VMEM] * (COUNT + 3) + [SMEM] + [VMEM] * (COUNT + 2) + [ANY],
        out_specs=ANY,
        input_output_aliases={2 * COUNT + 6: 0},
        scratch_shapes=[
            pltpu.VMEM((sum_rows(OUTER_PAIRS, LAG), WIDE), jnp.float32),
            pltpu.VMEM((len(OUTER_PAIRS), 3, LOOKS, COLS), jnp.float32),
            pltpu.SemaphoreType.DMA((len(OUTER_PAIRS),)),
        ],
        compiler_params=PARAMS,
        name="outer",
    )(*pieces, high, edges, power, pair_used, received, their_edges, *gathered, out)


def solution(mesh):
    return jax.shard_map(
        on_device,
        mesh=mesh,
        in_specs=(P("date", None, None, "col"), P("date"), P("date"), P("date", None)),
        out_specs=P("date", None, None, None, "col"),
        check_vma=False,
    )
```

time: 150 us -> 45.7 us (0.30)
  the two profiles are of different devices: /device:TPU:62 before, /device:TPU:94 now
where the time goes in v3:
time: 45.7 us; the launch traced here: 45.3 us
  waiting for transfers between devices  18.4 us (40%)
  starting transfers between devices  13 us (28%)
  Pallas kernels  9.78 us (21%)
  local copies, waits for them, and re-layouts  4.04 us (9%)
    ppermute x8, waiting for transfers between devices, permute(): return lax.ppermute(value, AXES, pairs)  18.4 us
    ppermute x8, starting transfers between devices, permute(): return lax.ppermute(value, AXES, pairs)  13 us
    unnamed x15, local copies, waits for them, and re-layouts  4.04 us
    pallas_call x1, Pallas kernels, on_device(): pl.pallas_call(inner, out_shape=[out_shape, f32(DATES - OUTER_FIRST, 8, C...  3.63 us
    pallas_call x1, Pallas kernels, on_device(): pl.pallas_call(prepare, out_shape=piece_shapes + [f32(LAG * AZ, 8, COLS),...  3.39 us
    pallas_call x1, Pallas kernels, on_device(): pl.pallas_call(outer, out_shape=out_shape, in_specs=[VMEM] * (COUNT + 3)...  2.76 us
  transfers between devices with their start and end apart: 8, of which 3 were waited for; matrix products, arithmetic and copies ran while one was open for 2% of the time, Pallas kernels for 8%

profile of v3, /device:TPU:94, one launch (start us, length us, event | category | flops | bytes accessed | tf_op | source)
XLA Modules:
  0.0 45.3 jit_solution(18056458733798453139)
XLA Ops:
  0.0 3.4 %prepare.1 = (f32[10,8,1024]{2,1,0:T(8,128)}, f32[10,8,1024]{2,1,0:T(8,128)}, f32[20,8,1024]{2,1,0:T(8,128)}, f32[2,5,8,128]{3,2,1,0:T(8,128)}, f32[2,5,8,128]{3,2,1,0:T(8,128)}) custom-call(f32[1920,128]{1,0:T(8,128)} %bitcast.5, s32[6]{0:T(128)} %refs_3_.1, s32[6]{0:T(128)} %refs_4_.1), custom_call_target="tpu_custom_call" | custom-call | tf_op jit(solution)/shard_map/prepare/pallas_call | solution.py:336
  3.4 0.7 %collective-permute-start.2 = (f32[10,8,1024]{2,1,0:T(8,128)}, f32[10,8,1024]{2,1,0:T(8,128)S(1)}, u32[]{:S(2)}, u32[]{:S(2)}) collective-permute-start(f32[10,8,1024]{2,1,0:T(8,128)} %get-tuple-element.16.refs_0_), channel_id=1, source_target_pairs={{256,256},{257,449},{258,258},{259,451},{260,276},{261,485},{262,2... | collective-permute-start | bytes 983048 | tf_op jit(solution)/shard_map/ppermute | solution.py:349
  4.1 0.7 %collective-permute-start.3 = (f32[10,8,1024]{2,1,0:T(8,128)}, f32[10,8,1024]{2,1,0:T(8,128)S(1)}, u32[]{:S(2)}, u32[]{:S(2)}) collective-permute-start(f32[10,8,1024]{2,1,0:T(8,128)} %get-tuple-element.17.refs_1_), channel_id=1, source_target_pairs={{256,304},{257,497},{258,306},{259,499},{260,324},{261,437},{262,3... | collective-permute-start | bytes 983048 | tf_op jit(solution)/shard_map/ppermute | solution.py:349
  4.8 2.8 %collective-permute-start.4 = (f32[20,8,1024]{2,1,0:T(8,128)}, f32[20,8,1024]{2,1,0:T(8,128)S(1)}, u32[]{:S(2)}, u32[]{:S(2)}) collective-permute-start(f32[20,8,1024]{2,1,0:T(8,128)} %get-tuple-element.23), channel_id=1, source_target_pairs={{16,0},{17,1},{18,2},{19,3},{20,4},{21,5},{22,6},{23,7},{24,8},{25... | collective-permute-start | bytes 1966088 | tf_op jit(solution)/shard_map/ppermute | solution.py:349
  7.6 1.9 %collective-permute-start = (f32[2,5,8,128]{3,2,1,0:T(8,128)}, f32[2,5,8,128]{3,2,1,0:T(8,128)S(1)}, u32[]{:S(2)}, u32[]{:S(2)}) collective-permute-start(f32[2,5,8,128]{3,2,1,0:T(8,128)} %get-tuple-element.18), channel_id=1, source_target_pairs={{1,0},{2,1},{3,2},{4,3},{5,4},{6,5},{7,6},{8,7},{9,8},{10,9},{11,1... | collective-permute-start | bytes 122888 | tf_op jit(solution)/shard_map/ppermute | solution.py:349
  9.5 2.4 %collective-permute-start.1 = (f32[2,5,8,128]{3,2,1,0:T(8,128)}, f32[2,5,8,128]{3,2,1,0:T(8,128)S(1)}, u32[]{:S(2)}, u32[]{:S(2)}) collective-permute-start(f32[2,5,8,128]{3,2,1,0:T(8,128)} %get-tuple-element.19), channel_id=1, source_target_pairs={{0,1},{1,2},{2,3},{3,4},{4,5},{5,6},{6,7},{7,8},{8,9},{9,10},{10,1... | collective-permute-start | bytes 122888 | tf_op jit(solution)/shard_map/ppermute | solution.py:349
  11.9 0.0 collective-permute-done
  11.9 3.1 %collective-permute-done.1 = f32[2,5,8,128]{3,2,1,0:T(8,128)S(1)} collective-permute-done((f32[2,5,8,128]{3,2,1,0:T(8,128)}, f32[2,5,8,128]{3,2,1,0:T(8,128)S(1)}, u32[]{:S(2)}, u32[]{:S(2)}) %collective-permute-start.1) | collective-permute-done | bytes 40992 | tf_op jit(solution)/shard_map/ppermute | solution.py:349
  15.0 0.0 collective-permute-done.2
  15.0 0.0 collective-permute-done.3
  15.0 1.3 %collective-permute-start.6 = (f32[10,8,1024]{2,1,0:T(8,128)S(1)}, f32[10,8,1024]{2,1,0:T(8,128)S(1)}, u32[]{:S(2)}, u32[]{:S(2)}) collective-permute-start(f32[10,8,1024]{2,1,0:T(8,128)S(1)} %collective-permute-done.2), channel_id=1, source_target_pairs={{256,240},{449,241},{258,242},{451,243},{276,244},{485,245},{278,2... | collective-permute-start | bytes 983048 | tf_op jit(solution)/shard_map/ppermute | solution.py:349
  16.3 1.3 %collective-permute-start.7 = (f32[10,8,1024]{2,1,0:T(8,128)S(1)}, f32[10,8,1024]{2,1,0:T(8,128)S(1)}, u32[]{:S(2)}, u32[]{:S(2)}) collective-permute-start(f32[10,8,1024]{2,1,0:T(8,128)S(1)} %collective-permute-done.3), channel_id=1, source_target_pairs={{304,240},{497,241},{306,242},{499,243},{324,244},{437,245},{326,2... | collective-permute-start | bytes 983048 | tf_op jit(solution)/shard_map/ppermute | solution.py:349
  17.7 1.9 %collective-permute-start.5 = (f32[1,5,8,128]{3,2,1,0:T(8,128)S(1)}, f32[1,5,8,128]{3,2,1,0:T(8,128)S(1)}, u32[]{:S(2)}, u32[]{:S(2)}) collective-permute-start(f32[1,5,8,128]{3,2,1,0:T(8,128)S(1)} %slice.3), channel_id=1, source_target_pairs={{16,0},{17,1},{18,2},{19,3},{20,4},{21,5},{22,6},{23,7},{24,8},{25... | collective-permute-start | bytes 61448 | tf_op jit(solution)/shard_map/ppermute | solution.py:349
  19.6 0.8 %copy.7.refs_6_.refs_5_ = s32[6,4]{1,0:T(8,128)S(1)} copy(s32[6,4]{0,1:T(4,128)} %param.7) | data formatting | bytes 192 | tf_op args[3]
  20.4 0.0 copy-done
  20.4 0.0 copy-start.1
  20.4 1.0 %copy-done.1 = f32[10,8,1024]{2,1,0:T(8,128)S(1)} copy-done((f32[10,8,1024]{2,1,0:T(8,128)S(1)}, f32[10,8,1024]{2,1,0:T(8,128)}, u32[]{:S(2)}) %copy-start.1) | copy-done | bytes 327704
  21.3 0.0 copy-start.3
  21.3 1.0 %copy-done.3 = f32[10,8,1024]{2,1,0:T(8,128)S(1)} copy-done((f32[10,8,1024]{2,1,0:T(8,128)S(1)}, f32[10,8,1024]{2,1,0:T(8,128)}, u32[]{:S(2)}) %copy-start.3) | copy-done | bytes 327704
  22.3 0.0 copy-start.5
  22.3 0.7 %copy-done.5 = s32[6]{0:T(128)S(1)} copy-done((s32[6]{0:T(128)S(1)}, s32[6]{0:T(128)}, u32[]{:S(2)}) %copy-start.5) | copy-done | bytes 48
  23.0 0.0 copy-start.6
  23.0 0.7 %copy-done.6 = s32[6]{0:T(128)S(1)} copy-done((s32[6]{0:T(128)S(1)}, s32[6]{0:T(128)}, u32[]{:S(2)}) %copy-start.6) | copy-done | bytes 48
  23.6 0.0 copy-start.2
  23.6 3.6 %inner.1 = (f32[6,4,3,4,1024]{4,3,2,1,0:T(4,128)}, f32[4,8,1024]{2,1,0:T(8,128)S(1)}, f32[2,5,8,1024]{3,2,1,0:T(8,128)S(1)}) custom-call(f32[10,8,1024]{2,1,0:T(8,128)S(1)} %copy-done.1, f32[10,8,1024]{2,1,0:T(8,128)S(1)} %copy-done.3, f32[1920,128]{1,0:T(8,128)S(1)} %bitcast.6, s32[6]{0:T(128)S(1)} %copy-done.5, s32[6]{0:T(128)S(1)} %copy-done.6, ...), custom_call_target="tpu_custom_call" | custom-call | tf_op jit(solution)/shard_map/inner/pallas_call | solution.py:368
  27.3 10.7 %collective-permute-done.5.refs_7_ = f32[1,5,8,128]{3,2,1,0:T(8,128)S(1)} collective-permute-done((f32[1,5,8,128]{3,2,1,0:T(8,128)S(1)}, f32[1,5,8,128]{3,2,1,0:T(8,128)S(1)}, u32[]{:S(2)}, u32[]{:S(2)}) %collective-permute-start.5) | collective-permute-done | bytes 20512 | tf_op jit(solution)/shard_map/ppermute | solution.py:349
  38.0 4.5 %collective-permute-done.6.refs_8_ = f32[10,8,1024]{2,1,0:T(8,128)S(1)} collective-permute-done((f32[10,8,1024]{2,1,0:T(8,128)S(1)}, f32[10,8,1024]{2,1,0:T(8,128)S(1)}, u32[]{:S(2)}, u32[]{:S(2)}) %collective-permute-start.6) | collective-permute-done | bytes 327712 | tf_op jit(solution)/shard_map/ppermute | solution.py:349
  42.5 0.0 collective-permute-done.7.refs_9_
  42.5 0.0 collective-permute-done.4.refs_6_
  42.5 0.0 copy-done.2
  42.5 0.0 copy-done.4
  42.5 2.8 %outer.1 = f32[6,4,3,4,1024]{4,3,2,1,0:T(4,128)} custom-call(f32[10,8,1024]{2,1,0:T(8,128)S(1)} %copy-done.2, f32[10,8,1024]{2,1,0:T(8,128)S(1)} %copy-done.4, f32[2,5,8,1024]{3,2,1,0:T(8,128)S(1)} %get-tuple-element.21.refs_2_, f32[2,5,8,128]{3,2,1,0:T(8,128)S(1)} %add.3.refs_5_.refs_3_, ...), custom_call_target="tpu_custom_call", output_to_operand_aliasing={{}: (10, {})} | custom-call | tf_op jit(solution)/shard_map/outer/pallas_call | solution.py:385
  (4 shorter events, 0.0 us)
Async XLA Ops:
  0.0 20.4 %copy-start = (f32[6,2,20,1024]{3,1,2,0:T(2,128)S(1)}, f32[6,2,20,1024]{3,1,2,0:T(2,128)}, u32[]{:S(2)}) copy-start(f32[6,2,20,1024]{3,1,2,0:T(2,128)} %param.4) | copy-start | bytes 2949124
  3.4 11.6 %collective-permute-start.2 = (f32[10,8,1024]{2,1,0:T(8,128)}, f32[10,8,1024]{2,1,0:T(8,128)S(1)}, u32[]{:S(2)}, u32[]{:S(2)}) collective-permute-start(f32[10,8,1024]{2,1,0:T(8,128)} %get-tuple-element.16.refs_0_), channel_id=1, source_target_pairs={{256,256},{257,449},{258,258},{259,451},{260,276},{261,485},{262,2... | collective-permute-start | bytes 983048 | tf_op jit(solution)/shard_map/ppermute | solution.py:349
  4.1 10.9 %collective-permute-start.3 = (f32[10,8,1024]{2,1,0:T(8,128)}, f32[10,8,1024]{2,1,0:T(8,128)S(1)}, u32[]{:S(2)}, u32[]{:S(2)}) collective-permute-start(f32[10,8,1024]{2,1,0:T(8,128)} %get-tuple-element.17.refs_1_), channel_id=1, source_target_pairs={{256,304},{257,497},{258,306},{259,499},{260,324},{261,437},{262,3... | collective-permute-start | bytes 983048 | tf_op jit(solution)/shard_map/ppermute | solution.py:349
  4.8 37.7 %collective-permute-start.4 = (f32[20,8,1024]{2,1,0:T(8,128)}, f32[20,8,1024]{2,1,0:T(8,128)S(1)}, u32[]{:S(2)}, u32[]{:S(2)}) collective-permute-start(f32[20,8,1024]{2,1,0:T(8,128)} %get-tuple-element.23), channel_id=1, source_target_pairs={{16,0},{17,1},{18,2},{19,3},{20,4},{21,5},{22,6},{23,7},{24,8},{25... | collective-permute-start | bytes 1966088 | tf_op jit(solution)/shard_map/ppermute | solution.py:349
  7.6 4.3 %collective-permute-start = (f32[2,5,8,128]{3,2,1,0:T(8,128)}, f32[2,5,8,128]{3,2,1,0:T(8,128)S(1)}, u32[]{:S(2)}, u32[]{:S(2)}) collective-permute-start(f32[2,5,8,128]{3,2,1,0:T(8,128)} %get-tuple-element.18), channel_id=1, source_target_pairs={{1,0},{2,1},{3,2},{4,3},{5,4},{6,5},{7,6},{8,7},{9,8},{10,9},{11,1... | collective-permute-start | bytes 122888 | tf_op jit(solution)/shard_map/ppermute | solution.py:349
  9.5 5.5 %collective-permute-start.1 = (f32[2,5,8,128]{3,2,1,0:T(8,128)}, f32[2,5,8,128]{3,2,1,0:T(8,128)S(1)}, u32[]{:S(2)}, u32[]{:S(2)}) collective-permute-start(f32[2,5,8,128]{3,2,1,0:T(8,128)} %get-tuple-element.19), channel_id=1, source_target_pairs={{0,1},{1,2},{2,3},{3,4},{4,5},{5,6},{6,7},{7,8},{8,9},{9,10},{10,1... | collective-permute-start | bytes 122888 | tf_op jit(solution)/shard_map/ppermute | solution.py:349
  15.0 27.4 %collective-permute-start.6 = (f32[10,8,1024]{2,1,0:T(8,128)S(1)}, f32[10,8,1024]{2,1,0:T(8,128)S(1)}, u32[]{:S(2)}, u32[]{:S(2)}) collective-permute-start(f32[10,8,1024]{2,1,0:T(8,128)S(1)} %collective-permute-done.2), channel_id=1, source_target_pairs={{256,240},{449,241},{258,242},{451,243},{276,244},{485,245},{278,2... | collective-permute-start | bytes 983048 | tf_op jit(solution)/shard_map/ppermute | solution.py:349
  16.3 26.1 %collective-permute-start.7 = (f32[10,8,1024]{2,1,0:T(8,128)S(1)}, f32[10,8,1024]{2,1,0:T(8,128)S(1)}, u32[]{:S(2)}, u32[]{:S(2)}) collective-permute-start(f32[10,8,1024]{2,1,0:T(8,128)S(1)} %collective-permute-done.3), channel_id=1, source_target_pairs={{304,240},{497,241},{306,242},{499,243},{324,244},{437,245},{326,2... | collective-permute-start | bytes 983048 | tf_op jit(solution)/shard_map/ppermute | solution.py:349
  17.7 20.3 %collective-permute-start.5 = (f32[1,5,8,128]{3,2,1,0:T(8,128)S(1)}, f32[1,5,8,128]{3,2,1,0:T(8,128)S(1)}, u32[]{:S(2)}, u32[]{:S(2)}) collective-permute-start(f32[1,5,8,128]{3,2,1,0:T(8,128)S(1)} %slice.3), channel_id=1, source_target_pairs={{16,0},{17,1},{18,2},{19,3},{20,4},{21,5},{22,6},{23,7},{24,8},{25... | collective-permute-start | bytes 61448 | tf_op jit(solution)/shard_map/ppermute | solution.py:349
  20.4 1.0 %copy-start.1 = (f32[10,8,1024]{2,1,0:T(8,128)S(1)}, f32[10,8,1024]{2,1,0:T(8,128)}, u32[]{:S(2)}) copy-start(f32[10,8,1024]{2,1,0:T(8,128)} %get-tuple-element.16.refs_0_) | copy-start | bytes 983044
  21.3 1.0 %copy-start.3 = (f32[10,8,1024]{2,1,0:T(8,128)S(1)}, f32[10,8,1024]{2,1,0:T(8,128)}, u32[]{:S(2)}) copy-start(f32[10,8,1024]{2,1,0:T(8,128)} %get-tuple-element.17.refs_1_) | copy-start | bytes 983044
  22.3 0.7 %copy-start.5 = (s32[6]{0:T(128)S(1)}, s32[6]{0:T(128)}, u32[]{:S(2)}) copy-start(s32[6]{0:T(128)} %refs_3_.1) | copy-start | bytes 76
  23.0 0.7 %copy-start.6 = (s32[6]{0:T(128)S(1)}, s32[6]{0:T(128)}, u32[]{:S(2)}) copy-start(s32[6]{0:T(128)} %refs_4_.1) | copy-start | bytes 76
  23.6 18.9 %copy-start.2 = (f32[10,8,1024]{2,1,0:T(8,128)S(1)}, f32[10,8,1024]{2,1,0:T(8,128)}, u32[]{:S(2)}) copy-start(f32[10,8,1024]{2,1,0:T(8,128)} %get-tuple-element.16.refs_0_) | copy-start | bytes 983044
  23.6 18.9 %copy-start.4 = (f32[10,8,1024]{2,1,0:T(8,128)S(1)}, f32[10,8,1024]{2,1,0:T(8,128)}, u32[]{:S(2)}) copy-start(f32[10,8,1024]{2,1,0:T(8,128)} %get-tuple-element.17.refs_1_) | copy-start | bytes 983044

commit v4 on v3

--- a/solution.py
+++ b/solution.py
@@ -45,6 +45,14 @@
 
 def f32(*shape):
     return jax.ShapeDtypeStruct(shape, jnp.float32)
+
+
+def f32_vmem(*shape):
+    return pltpu.VMEM(shape, jnp.float32)
+
+
+def in_hbm(x):
+    return pltpu.with_memory_space_constraint(x, pltpu.HBM)
 
 
 def lane_roll(x, by):
@@ -247,7 +255,7 @@
                 result[8 * n : 8 * n + 8],
                 powers[i],
                 powers[i + k + 1],
-                used[i, k].astype(jnp.float32),
+                used[k, i].astype(jnp.float32),
             )
 
 
@@ -297,7 +305,7 @@
                 result[8 * n : 8 * n + 8],
                 power[i - OUTER_FIRST, :, lanes],
                 powers[i + k + 1 - DATES],
-                used[i, k].astype(jnp.float32),
+                used[k, i].astype(jnp.float32),
             )
     copies = [
         pltpu.make_async_copy(staged.at[n], out.at[i, k], sems.at[n])
@@ -331,19 +339,20 @@
 def on_device(slc, first_row, stop_row, pair_used):
     slc = slc.reshape(DATES, 2, AZ * LOOKS, CHUNKS, LANES).transpose(0, 2, 3, 1, 4)
     slc = slc.reshape(DATES * PER_DATE, LANES)
-    piece_shapes = [f32(size, 8, COLS) for size in PIECES]
-    edge_shape = f32(2, AZ, 8, LANES)
+    piece_shapes = [f32_vmem(size, 8, COLS) for size in PIECES]
+    edge_shape = f32_vmem(2, AZ, 8, LANES)
     *pieces, low, edge_low, edge_high = pl.pallas_call(
         prepare,
-        out_shape=piece_shapes + [f32(LAG * AZ, 8, COLS), edge_shape, edge_shape],
+        out_shape=piece_shapes + [f32_vmem(LAG * AZ, 8, COLS), edge_shape, edge_shape],
         in_specs=[ANY, SMEM, SMEM],
         out_specs=[VMEM] * (COUNT + 3),
         scratch_shapes=[
             pltpu.VMEM((DATES * PER_DATE, LANES), jnp.float32),
             pltpu.SemaphoreType.DMA((DATES,)),
         ],
+        compiler_params=PARAMS,
         name="prepare",
-    )(slc, first_row, stop_row)
+    )(in_hbm(slc), in_hbm(first_row), in_hbm(stop_row))
 
     def permute(value, pairs):
         return lax.ppermute(value, AXES, pairs)
@@ -360,17 +369,18 @@
     left = permute(edge_high, to_right)
     right = permute(edge_low, to_left)
     received = permute(low, near)
-    edges, *scattered = lax.optimization_barrier((right + left, *scattered))
+    edges = right + left
     gathered = [permute(piece, pairs) for piece, pairs in zip(scattered, gather)]
     their_edges = permute(edges[:1], near + far)
 
+    used = pair_used.T
     out_shape = f32(DATES, LAG, 3, LOOKS, COLS)
     out, power, high = pl.pallas_call(
         inner,
         out_shape=[
             out_shape,
-            f32(DATES - OUTER_FIRST, 8, COLS),
-            f32(DATES - LAG, AZ, 8, COLS),
+            f32_vmem(DATES - OUTER_FIRST, 8, COLS),
+            f32_vmem(DATES - LAG, AZ, 8, COLS),
         ],
         in_specs=[VMEM] * COUNT + [ANY, SMEM, SMEM, VMEM, SMEM],
         out_specs=[VMEM] * 3,
@@ -381,7 +391,7 @@
         ],
         compiler_params=PARAMS,
         name="inner",
-    )(*pieces, slc, first_row, stop_row, edges, pair_used)
+    )(*pieces, in_hbm(slc), in_hbm(first_row), in_hbm(stop_row), edges, in_hbm(used))
     return pl.pallas_call(
         outer,
         out_shape=out_shape,
@@ -395,7 +405,7 @@
         ],
         compiler_params=PARAMS,
         name="outer",
-    )(*pieces, high, edges, power, pair_used, received, their_edges, *gathered, out)
+    )(*pieces, high, edges, power, in_hbm(used), received, their_edges, *gathered, out)
 
 
 def solution(mesh):

time: 45.7 us -> 43.7 us (0.956)
  the two profiles are of different devices: /device:TPU:94 before, /device:TPU:62 now
where the time goes in v4:
time: 43.7 us; the launch traced here: 43.4 us
  waiting for transfers between devices  21 us (48%)
  starting transfers between devices  13 us (30%)
  Pallas kernels  9.34 us (21%)
    ppermute x8, waiting for transfers between devices, permute(): return lax.ppermute(value, AXES, pairs)  21 us
    ppermute x8, starting transfers between devices, permute(): return lax.ppermute(value, AXES, pairs)  13 us
    pallas_call x1, Pallas kernels, on_device(): pl.pallas_call(inner, out_shape=[out_shape, f32_vmem(DATES - OUTER_FIRST,...  4.22 us
    pallas_call x1, Pallas kernels, on_device(): pl.pallas_call(outer, out_shape=out_shape, in_specs=[VMEM] * (COUNT + 3)...  2.85 us
    pallas_call x1, Pallas kernels, on_device(): pl.pallas_call(prepare, out_shape=piece_shapes + [f32_vmem(LAG * AZ, 8, C...  2.27 us
  transfers between devices with their start and end apart: 8, of which 2 were waited for; matrix products, arithmetic and copies ran while one was open for 0% of the time, Pallas kernels for 10%

profile of v4, /device:TPU:62, one launch (start us, length us, event | category | flops | bytes accessed | tf_op | source)
XLA Modules:
  0.0 43.4 jit_solution(11761893730775699051)
XLA Ops:
  0.0 2.3 %prepare.1 = (f32[10,8,1024]{2,1,0:T(8,128)S(1)}, f32[10,8,1024]{2,1,0:T(8,128)S(1)}, f32[20,8,1024]{2,1,0:T(8,128)S(1)}, f32[2,5,8,128]{3,2,1,0:T(8,128)S(1)}, f32[2,5,8,128]{3,2,1,0:T(8,128)S(1)}) custom-call(f32[1920,128]{1,0:T(8,128)} %bitcast.6, s32[6]{0:T(128)} %refs_3_.1, s32[6]{0:T(128)} %refs_4_.1), custom_call_target="tpu_custom_call" | custom-call | tf_op jit(solution)/shard_map/prepare/pallas_call | solution.py:344
  2.3 0.7 %collective-permute-start.4 = (f32[10,8,1024]{2,1,0:T(8,128)S(1)}, f32[10,8,1024]{2,1,0:T(8,128)S(1)}, u32[]{:S(2)}, u32[]{:S(2)}) collective-permute-start(f32[10,8,1024]{2,1,0:T(8,128)S(1)} %get-tuple-element.13.refs_0_), channel_id=1, source_target_pairs={{256,256},{257,449},{258,258},{259,451},{260,276},{261,485},{262,2... | collective-permute-start | bytes 983048 | tf_op jit(solution)/shard_map/ppermute | solution.py:358
  3.0 0.7 %collective-permute-start.6 = (f32[10,8,1024]{2,1,0:T(8,128)S(1)}, f32[10,8,1024]{2,1,0:T(8,128)S(1)}, u32[]{:S(2)}, u32[]{:S(2)}) collective-permute-start(f32[10,8,1024]{2,1,0:T(8,128)S(1)} %get-tuple-element.14.refs_1_), channel_id=1, source_target_pairs={{256,304},{257,497},{258,306},{259,499},{260,324},{261,437},{262,3... | collective-permute-start | bytes 983048 | tf_op jit(solution)/shard_map/ppermute | solution.py:358
  3.7 2.8 %collective-permute-start.2 = (f32[20,8,1024]{2,1,0:T(8,128)S(1)}, f32[20,8,1024]{2,1,0:T(8,128)S(1)}, u32[]{:S(2)}, u32[]{:S(2)}) collective-permute-start(f32[20,8,1024]{2,1,0:T(8,128)S(1)} %get-tuple-element.19), channel_id=1, source_target_pairs={{16,0},{17,1},{18,2},{19,3},{20,4},{21,5},{22,6},{23,7},{24,8},{25... | collective-permute-start | bytes 1966088 | tf_op jit(solution)/shard_map/ppermute | solution.py:358
  6.4 0.0 collective-permute-done.4
  6.5 1.3 %collective-permute-start.5 = (f32[10,8,1024]{2,1,0:T(8,128)S(1)}, f32[10,8,1024]{2,1,0:T(8,128)S(1)}, u32[]{:S(2)}, u32[]{:S(2)}) collective-permute-start(f32[10,8,1024]{2,1,0:T(8,128)S(1)} %collective-permute-done.4), channel_id=1, source_target_pairs={{256,240},{449,241},{258,242},{451,243},{276,244},{485,245},{278,2... | collective-permute-start | bytes 983048 | tf_op jit(solution)/shard_map/ppermute | solution.py:358
  7.8 0.0 collective-permute-done.6
  7.8 1.3 %collective-permute-start.7 = (f32[10,8,1024]{2,1,0:T(8,128)S(1)}, f32[10,8,1024]{2,1,0:T(8,128)S(1)}, u32[]{:S(2)}, u32[]{:S(2)}) collective-permute-start(f32[10,8,1024]{2,1,0:T(8,128)S(1)} %collective-permute-done.6), channel_id=1, source_target_pairs={{304,240},{497,241},{306,242},{499,243},{324,244},{437,245},{326,2... | collective-permute-start | bytes 983048 | tf_op jit(solution)/shard_map/ppermute | solution.py:358
  9.1 1.9 %collective-permute-start = (f32[2,5,8,128]{3,2,1,0:T(8,128)S(1)}, f32[2,5,8,128]{3,2,1,0:T(8,128)S(1)}, u32[]{:S(2)}, u32[]{:S(2)}) collective-permute-start(f32[2,5,8,128]{3,2,1,0:T(8,128)S(1)} %get-tuple-element.15), channel_id=1, source_target_pairs={{1,0},{2,1},{3,2},{4,3},{5,4},{6,5},{7,6},{8,7},{9,8},{10,9},{11,1... | collective-permute-start | bytes 122888 | tf_op jit(solution)/shard_map/ppermute | solution.py:358
  11.0 2.4 %collective-permute-start.1 = (f32[2,5,8,128]{3,2,1,0:T(8,128)S(1)}, f32[2,5,8,128]{3,2,1,0:T(8,128)S(1)}, u32[]{:S(2)}, u32[]{:S(2)}) collective-permute-start(f32[2,5,8,128]{3,2,1,0:T(8,128)S(1)} %get-tuple-element.16), channel_id=1, source_target_pairs={{0,1},{1,2},{2,3},{3,4},{4,5},{5,6},{6,7},{7,8},{8,9},{9,10},{10,1... | collective-permute-start | bytes 122888 | tf_op jit(solution)/shard_map/ppermute | solution.py:358
  13.4 0.0 collective-permute-done
  13.4 2.9 %collective-permute-done.1 = f32[2,5,8,128]{3,2,1,0:T(8,128)S(1)} collective-permute-done((f32[2,5,8,128]{3,2,1,0:T(8,128)S(1)}, f32[2,5,8,128]{3,2,1,0:T(8,128)S(1)}, u32[]{:S(2)}, u32[]{:S(2)}) %collective-permute-start.1) | collective-permute-done | bytes 40992 | tf_op jit(solution)/shard_map/ppermute | solution.py:358
  16.3 1.9 %collective-permute-start.3 = (f32[1,5,8,128]{3,2,1,0:T(8,128)S(1)}, f32[1,5,8,128]{3,2,1,0:T(8,128)S(1)}, u32[]{:S(2)}, u32[]{:S(2)}) collective-permute-start(f32[1,5,8,128]{3,2,1,0:T(8,128)S(1)} %slice.4), channel_id=1, source_target_pairs={{16,0},{17,1},{18,2},{19,3},{20,4},{21,5},{22,6},{23,7},{24,8},{25... | collective-permute-start | bytes 61448 | tf_op jit(solution)/shard_map/ppermute | solution.py:358
  18.3 4.2 %inner.1 = (f32[6,4,3,4,1024]{4,3,2,1,0:T(4,128)}, f32[4,8,1024]{2,1,0:T(8,128)S(1)}, f32[2,5,8,1024]{3,2,1,0:T(8,128)S(1)}) custom-call(f32[10,8,1024]{2,1,0:T(8,128)S(1)} %get-tuple-element.13.refs_0_, f32[10,8,1024]{2,1,0:T(8,128)S(1)} %get-tuple-element.14.refs_1_, f32[1920,128]{1,0:T(8,128)} %bitcast.7, s32[6]{0:T(128)} %refs_3_.1, s32[6]{0:T(128)} %refs_4_.1, ...), custom_call_target="tpu_custom_call" | custom-call | tf_op jit(solution)/shard_map/inner/pallas_call | solution.py:378
  22.5 18.1 %collective-permute-done.3.refs_7_ = f32[1,5,8,128]{3,2,1,0:T(8,128)S(1)} collective-permute-done((f32[1,5,8,128]{3,2,1,0:T(8,128)S(1)}, f32[1,5,8,128]{3,2,1,0:T(8,128)S(1)}, u32[]{:S(2)}, u32[]{:S(2)}) %collective-permute-start.3) | collective-permute-done | bytes 20512 | tf_op jit(solution)/shard_map/ppermute | solution.py:358
  40.5 0.0 collective-permute-done.5.refs_8_
  40.5 0.0 collective-permute-done.7.refs_9_
  40.5 0.0 collective-permute-done.2.refs_6_
  40.5 2.9 %outer.1 = f32[6,4,3,4,1024]{4,3,2,1,0:T(4,128)} custom-call(f32[10,8,1024]{2,1,0:T(8,128)S(1)} %get-tuple-element.13.refs_0_, f32[10,8,1024]{2,1,0:T(8,128)S(1)} %get-tuple-element.14.refs_1_, f32[2,5,8,1024]{3,2,1,0:T(8,128)S(1)} %get-tuple-element.17.refs_2_, f32[2,5,8,128]{3,2,1,0:T(8,128)S(1)} %add.3.refs_5_.refs_3_, ...), custom_call_target="tpu_custom_call", output_to_operand_aliasing={{}: (10, {})} | custom-call | tf_op jit(solution)/shard_map/outer/pallas_call | solution.py:395
  (2 shorter events, 0.0 us)
Async XLA Ops:
  2.3 4.2 %collective-permute-start.4 = (f32[10,8,1024]{2,1,0:T(8,128)S(1)}, f32[10,8,1024]{2,1,0:T(8,128)S(1)}, u32[]{:S(2)}, u32[]{:S(2)}) collective-permute-start(f32[10,8,1024]{2,1,0:T(8,128)S(1)} %get-tuple-element.13.refs_0_), channel_id=1, source_target_pairs={{256,256},{257,449},{258,258},{259,451},{260,276},{261,485},{262,2... | collective-permute-start | bytes 983048 | tf_op jit(solution)/shard_map/ppermute | solution.py:358
  3.0 4.8 %collective-permute-start.6 = (f32[10,8,1024]{2,1,0:T(8,128)S(1)}, f32[10,8,1024]{2,1,0:T(8,128)S(1)}, u32[]{:S(2)}, u32[]{:S(2)}) collective-permute-start(f32[10,8,1024]{2,1,0:T(8,128)S(1)} %get-tuple-element.14.refs_1_), channel_id=1, source_target_pairs={{256,304},{257,497},{258,306},{259,499},{260,324},{261,437},{262,3... | collective-permute-start | bytes 983048 | tf_op jit(solution)/shard_map/ppermute | solution.py:358
  3.7 36.9 %collective-permute-start.2 = (f32[20,8,1024]{2,1,0:T(8,128)S(1)}, f32[20,8,1024]{2,1,0:T(8,128)S(1)}, u32[]{:S(2)}, u32[]{:S(2)}) collective-permute-start(f32[20,8,1024]{2,1,0:T(8,128)S(1)} %get-tuple-element.19), channel_id=1, source_target_pairs={{16,0},{17,1},{18,2},{19,3},{20,4},{21,5},{22,6},{23,7},{24,8},{25... | collective-permute-start | bytes 1966088 | tf_op jit(solution)/shard_map/ppermute | solution.py:358
  6.5 34.1 %collective-permute-start.5 = (f32[10,8,1024]{2,1,0:T(8,128)S(1)}, f32[10,8,1024]{2,1,0:T(8,128)S(1)}, u32[]{:S(2)}, u32[]{:S(2)}) collective-permute-start(f32[10,8,1024]{2,1,0:T(8,128)S(1)} %collective-permute-done.4), channel_id=1, source_target_pairs={{256,240},{449,241},{258,242},{451,243},{276,244},{485,245},{278,2... | collective-permute-start | bytes 983048 | tf_op jit(solution)/shard_map/ppermute | solution.py:358
  7.8 32.8 %collective-permute-start.7 = (f32[10,8,1024]{2,1,0:T(8,128)S(1)}, f32[10,8,1024]{2,1,0:T(8,128)S(1)}, u32[]{:S(2)}, u32[]{:S(2)}) collective-permute-start(f32[10,8,1024]{2,1,0:T(8,128)S(1)} %collective-permute-done.6), channel_id=1, source_target_pairs={{304,240},{497,241},{306,242},{499,243},{324,244},{437,245},{326,2... | collective-permute-start | bytes 983048 | tf_op jit(solution)/shard_map/ppermute | solution.py:358
  9.1 4.3 %collective-permute-start = (f32[2,5,8,128]{3,2,1,0:T(8,128)S(1)}, f32[2,5,8,128]{3,2,1,0:T(8,128)S(1)}, u32[]{:S(2)}, u32[]{:S(2)}) collective-permute-start(f32[2,5,8,128]{3,2,1,0:T(8,128)S(1)} %get-tuple-element.15), channel_id=1, source_target_pairs={{1,0},{2,1},{3,2},{4,3},{5,4},{6,5},{7,6},{8,7},{9,8},{10,9},{11,1... | collective-permute-start | bytes 122888 | tf_op jit(solution)/shard_map/ppermute | solution.py:358
  11.0 5.3 %collective-permute-start.1 = (f32[2,5,8,128]{3,2,1,0:T(8,128)S(1)}, f32[2,5,8,128]{3,2,1,0:T(8,128)S(1)}, u32[]{:S(2)}, u32[]{:S(2)}) collective-permute-start(f32[2,5,8,128]{3,2,1,0:T(8,128)S(1)} %get-tuple-element.16), channel_id=1, source_target_pairs={{0,1},{1,2},{2,3},{3,4},{4,5},{5,6},{6,7},{7,8},{8,9},{9,10},{10,1... | collective-permute-start | bytes 122888 | tf_op jit(solution)/shard_map/ppermute | solution.py:358
  16.3 24.2 %collective-permute-start.3 = (f32[1,5,8,128]{3,2,1,0:T(8,128)S(1)}, f32[1,5,8,128]{3,2,1,0:T(8,128)S(1)}, u32[]{:S(2)}, u32[]{:S(2)}) collective-permute-start(f32[1,5,8,128]{3,2,1,0:T(8,128)S(1)} %slice.4), channel_id=1, source_target_pairs={{16,0},{17,1},{18,2},{19,3},{20,4},{21,5},{22,6},{23,7},{24,8},{25... | collective-permute-start | bytes 61448 | tf_op jit(solution)/shard_map/ppermute | solution.py:358

commit v5 on v4

--- a/solution.py
+++ b/solution.py
@@ -25,10 +25,10 @@
 COUNT = len(PIECES)
 STARTS = [sum(PIECES[:n]) for n in range(COUNT)]
 COLUMN_SETS = (
-    (((0, 0), (3, 0)), ((0, 3), (3, 3))),
-    (((1, 0), (0, 1)), ((2, 3), (3, 2))),
-    (((2, 0), (0, 2)), ((1, 3), (3, 1))),
-    (((1, 1), (2, 2)), ((2, 1), (1, 2))),
+    (None, ((3, 0), (1, 3))),
+    (((0, 3), (3, 1)), ((1, 0), (0, 1))),
+    (((0, 1), (1, 0)), ((2, 0), (0, 3))),
+    (((0, 2), (3, 0)), ((1, 1), (2, 0))),
 )
 SOURCE_XY = (0, 0)
 TARGET_XY = (3, 3)
@@ -321,15 +321,19 @@
     def flat(x, y, z, core):
         return ((z // 8) * 16 + y * 4 + x) * 16 + (z % 8) * 2 + core
 
+    straight = []
     scatter = [[] for _ in PIECES]
     gather = [[] for _ in PIECES]
     for z in range(8):
         for core in range(2):
+            if COLUMN_SETS[z // 2][core] is None:
+                straight.append((flat(*SOURCE_XY, 8 + z, core), flat(*TARGET_XY, z, core)))
+                continue
             for n, (x, y) in enumerate(COLUMN_SETS[z // 2][core]):
                 relay = flat(x, y, 8 + z, core)
                 scatter[n].append((flat(*SOURCE_XY, 8 + z, core), relay))
                 gather[n].append((relay, flat(*TARGET_XY, z, core)))
-    return scatter, gather
+    return straight, scatter, gather
 
 
 def sum_rows(pairs, dates):
@@ -363,12 +367,12 @@
     far = [(16 * 16 + c, 15 * 16 + c) for c in range(16)]
     to_right = [(d * 16 + c, d * 16 + c + 1) for d in range(32) for c in range(15)]
     to_left = [(b, a) for a, b in to_right]
-    scatter, gather = far_permutes()
+    straight, scatter, gather = far_permutes()
 
     scattered = [permute(piece, pairs) for piece, pairs in zip(pieces, scatter)]
     left = permute(edge_high, to_right)
     right = permute(edge_low, to_left)
-    received = permute(low, near)
+    received = permute(low, near + straight)
     edges = right + left
     gathered = [permute(piece, pairs) for piece, pairs in zip(scattered, gather)]
     their_edges = permute(edges[:1], near + far)

time: 43.7 us -> 40.3 us (0.922)
  waiting for transfers between devices: 21 us -> 18.4 us
  starting transfers between devices: 13 us -> 12 us
    ppermute x8, waiting for transfers between devices: 21 us -> 18.4 us  [permute(): return lax.ppermute(value, AXES, pairs)]
    ppermute x8, starting transfers between devices: 13 us -> 12 us  [permute(): return lax.ppermute(value, AXES, pairs)]
  transfers between devices with their start and end apart: 8 -> 8, of which waited for: 2 -> 2; matrix products, arithmetic and copies ran while one was open for 0% -> 0% of each run, Pallas kernels for 10% -> 11%
where the time goes in v5:
time: 40.3 us; the launch traced here: 39.9 us
  waiting for transfers between devices  18.4 us (46%)
  starting transfers between devices  12 us (30%)
  Pallas kernels  9.34 us (23%)
    ppermute x8, waiting for transfers between devices, permute(): return lax.ppermute(value, AXES, pairs)  18.4 us
    ppermute x8, starting transfers between devices, permute(): return lax.ppermute(value, AXES, pairs)  12 us
    pallas_call x1, Pallas kernels, on_device(): pl.pallas_call(inner, out_shape=[out_shape, f32_vmem(DATES - OUTER_FIRST,...  4.22 us
    pallas_call x1, Pallas kernels, on_device(): pl.pallas_call(outer, out_shape=out_shape, in_specs=[VMEM] * (COUNT + 3)...  2.85 us
    pallas_call x1, Pallas kernels, on_device(): pl.pallas_call(prepare, out_shape=piece_shapes + [f32_vmem(LAG * AZ, 8, C...  2.27 us
  transfers between devices with their start and end apart: 8, of which 2 were waited for; matrix products, arithmetic and copies ran while one was open for 0% of the time, Pallas kernels for 11%

profile of v5, /device:TPU:62, one launch (start us, length us, event | category | flops | bytes accessed | tf_op | source)
XLA Modules:
  0.0 39.9 jit_solution(16450841471982100717)
XLA Ops:
  0.0 2.3 %prepare.1 = (f32[10,8,1024]{2,1,0:T(8,128)S(1)}, f32[10,8,1024]{2,1,0:T(8,128)S(1)}, f32[20,8,1024]{2,1,0:T(8,128)S(1)}, f32[2,5,8,128]{3,2,1,0:T(8,128)S(1)}, f32[2,5,8,128]{3,2,1,0:T(8,128)S(1)}) custom-call(f32[1920,128]{1,0:T(8,128)} %bitcast.6, s32[6]{0:T(128)} %refs_3_.1, s32[6]{0:T(128)} %refs_4_.1), custom_call_target="tpu_custom_call" | custom-call | tf_op jit(solution)/shard_map/prepare/pallas_call | solution.py:348
  2.3 0.7 %collective-permute-start.4 = (f32[10,8,1024]{2,1,0:T(8,128)S(1)}, f32[10,8,1024]{2,1,0:T(8,128)S(1)}, u32[]{:S(2)}, u32[]{:S(2)}) collective-permute-start(f32[10,8,1024]{2,1,0:T(8,128)S(1)} %get-tuple-element.13.refs_0_), channel_id=1, source_target_pairs={{257,305},{259,307},{260,452},{261,277},{262,454},{263,279},{264,3... | collective-permute-start | bytes 983048 | tf_op jit(solution)/shard_map/ppermute | solution.py:362
  3.0 0.7 %collective-permute-start.6 = (f32[10,8,1024]{2,1,0:T(8,128)S(1)}, f32[10,8,1024]{2,1,0:T(8,128)S(1)}, u32[]{:S(2)}, u32[]{:S(2)}) collective-permute-start(f32[10,8,1024]{2,1,0:T(8,128)S(1)} %get-tuple-element.14.refs_1_), channel_id=1, source_target_pairs={{257,465},{259,467},{260,372},{261,325},{262,374},{263,327},{264,2... | collective-permute-start | bytes 983048 | tf_op jit(solution)/shard_map/ppermute | solution.py:362
  3.7 2.7 %collective-permute-start.2 = (f32[20,8,1024]{2,1,0:T(8,128)S(1)}, f32[20,8,1024]{2,1,0:T(8,128)S(1)}, u32[]{:S(2)}, u32[]{:S(2)}) collective-permute-start(f32[20,8,1024]{2,1,0:T(8,128)S(1)} %get-tuple-element.19), channel_id=1, source_target_pairs={{16,0},{17,1},{18,2},{19,3},{20,4},{21,5},{22,6},{23,7},{24,8},{25... | collective-permute-start | bytes 1966088 | tf_op jit(solution)/shard_map/ppermute | solution.py:362
  6.4 0.0 collective-permute-done.4
  6.4 0.7 %collective-permute-start.5 = (f32[10,8,1024]{2,1,0:T(8,128)S(1)}, f32[10,8,1024]{2,1,0:T(8,128)S(1)}, u32[]{:S(2)}, u32[]{:S(2)}) collective-permute-start(f32[10,8,1024]{2,1,0:T(8,128)S(1)} %collective-permute-done.4), channel_id=1, source_target_pairs={{305,241},{307,243},{452,244},{277,245},{454,246},{279,247},{328,2... | collective-permute-start | bytes 983048 | tf_op jit(solution)/shard_map/ppermute | solution.py:362
  7.1 0.0 collective-permute-done.6
  7.1 0.7 %collective-permute-start.7 = (f32[10,8,1024]{2,1,0:T(8,128)S(1)}, f32[10,8,1024]{2,1,0:T(8,128)S(1)}, u32[]{:S(2)}, u32[]{:S(2)}) collective-permute-start(f32[10,8,1024]{2,1,0:T(8,128)S(1)} %collective-permute-done.6), channel_id=1, source_target_pairs={{465,241},{467,243},{372,244},{325,245},{374,246},{327,247},{280,2... | collective-permute-start | bytes 983048 | tf_op jit(solution)/shard_map/ppermute | solution.py:362
  7.8 2.4 %collective-permute-start = (f32[2,5,8,128]{3,2,1,0:T(8,128)S(1)}, f32[2,5,8,128]{3,2,1,0:T(8,128)S(1)}, u32[]{:S(2)}, u32[]{:S(2)}) collective-permute-start(f32[2,5,8,128]{3,2,1,0:T(8,128)S(1)} %get-tuple-element.15), channel_id=1, source_target_pairs={{1,0},{2,1},{3,2},{4,3},{5,4},{6,5},{7,6},{8,7},{9,8},{10,9},{11,1... | collective-permute-start | bytes 122888 | tf_op jit(solution)/shard_map/ppermute | solution.py:362
  10.2 2.2 %collective-permute-start.1 = (f32[2,5,8,128]{3,2,1,0:T(8,128)S(1)}, f32[2,5,8,128]{3,2,1,0:T(8,128)S(1)}, u32[]{:S(2)}, u32[]{:S(2)}) collective-permute-start(f32[2,5,8,128]{3,2,1,0:T(8,128)S(1)} %get-tuple-element.16), channel_id=1, source_target_pairs={{0,1},{1,2},{2,3},{3,4},{4,5},{5,6},{6,7},{7,8},{8,9},{9,10},{10,1... | collective-permute-start | bytes 122888 | tf_op jit(solution)/shard_map/ppermute | solution.py:362
  12.5 0.0 collective-permute-done
  12.5 3.1 %collective-permute-done.1 = f32[2,5,8,128]{3,2,1,0:T(8,128)S(1)} collective-permute-done((f32[2,5,8,128]{3,2,1,0:T(8,128)S(1)}, f32[2,5,8,128]{3,2,1,0:T(8,128)S(1)}, u32[]{:S(2)}, u32[]{:S(2)}) %collective-permute-start.1) | collective-permute-done | bytes 40992 | tf_op jit(solution)/shard_map/ppermute | solution.py:362
  15.6 1.9 %collective-permute-start.3 = (f32[1,5,8,128]{3,2,1,0:T(8,128)S(1)}, f32[1,5,8,128]{3,2,1,0:T(8,128)S(1)}, u32[]{:S(2)}, u32[]{:S(2)}) collective-permute-start(f32[1,5,8,128]{3,2,1,0:T(8,128)S(1)} %slice.4), channel_id=1, source_target_pairs={{16,0},{17,1},{18,2},{19,3},{20,4},{21,5},{22,6},{23,7},{24,8},{25... | collective-permute-start | bytes 61448 | tf_op jit(solution)/shard_map/ppermute | solution.py:362
  17.5 4.2 %inner.1 = (f32[6,4,3,4,1024]{4,3,2,1,0:T(4,128)}, f32[4,8,1024]{2,1,0:T(8,128)S(1)}, f32[2,5,8,1024]{3,2,1,0:T(8,128)S(1)}) custom-call(f32[10,8,1024]{2,1,0:T(8,128)S(1)} %get-tuple-element.13.refs_0_, f32[10,8,1024]{2,1,0:T(8,128)S(1)} %get-tuple-element.14.refs_1_, f32[1920,128]{1,0:T(8,128)} %bitcast.7, s32[6]{0:T(128)} %refs_3_.1, s32[6]{0:T(128)} %refs_4_.1, ...), custom_call_target="tpu_custom_call" | custom-call | tf_op jit(solution)/shard_map/inner/pallas_call | solution.py:382
  21.8 15.3 %collective-permute-done.3.refs_7_ = f32[1,5,8,128]{3,2,1,0:T(8,128)S(1)} collective-permute-done((f32[1,5,8,128]{3,2,1,0:T(8,128)S(1)}, f32[1,5,8,128]{3,2,1,0:T(8,128)S(1)}, u32[]{:S(2)}, u32[]{:S(2)}) %collective-permute-start.3) | collective-permute-done | bytes 20512 | tf_op jit(solution)/shard_map/ppermute | solution.py:362
  37.1 0.0 collective-permute-done.5.refs_8_
  37.1 0.0 collective-permute-done.7.refs_9_
  37.1 0.0 collective-permute-done.2.refs_6_
  37.1 2.8 %outer.1 = f32[6,4,3,4,1024]{4,3,2,1,0:T(4,128)} custom-call(f32[10,8,1024]{2,1,0:T(8,128)S(1)} %get-tuple-element.13.refs_0_, f32[10,8,1024]{2,1,0:T(8,128)S(1)} %get-tuple-element.14.refs_1_, f32[2,5,8,1024]{3,2,1,0:T(8,128)S(1)} %get-tuple-element.17.refs_2_, f32[2,5,8,128]{3,2,1,0:T(8,128)S(1)} %add.3.refs_5_.refs_3_, ...), custom_call_target="tpu_custom_call", output_to_operand_aliasing={{}: (10, {})} | custom-call | tf_op jit(solution)/shard_map/outer/pallas_call | solution.py:399
  (2 shorter events, 0.0 us)
Async XLA Ops:
  2.3 4.1 %collective-permute-start.4 = (f32[10,8,1024]{2,1,0:T(8,128)S(1)}, f32[10,8,1024]{2,1,0:T(8,128)S(1)}, u32[]{:S(2)}, u32[]{:S(2)}) collective-permute-start(f32[10,8,1024]{2,1,0:T(8,128)S(1)} %get-tuple-element.13.refs_0_), channel_id=1, source_target_pairs={{257,305},{259,307},{260,452},{261,277},{262,454},{263,279},{264,3... | collective-permute-start | bytes 983048 | tf_op jit(solution)/shard_map/ppermute | solution.py:362
  3.0 4.1 %collective-permute-start.6 = (f32[10,8,1024]{2,1,0:T(8,128)S(1)}, f32[10,8,1024]{2,1,0:T(8,128)S(1)}, u32[]{:S(2)}, u32[]{:S(2)}) collective-permute-start(f32[10,8,1024]{2,1,0:T(8,128)S(1)} %get-tuple-element.14.refs_1_), channel_id=1, source_target_pairs={{257,465},{259,467},{260,372},{261,325},{262,374},{263,327},{264,2... | collective-permute-start | bytes 983048 | tf_op jit(solution)/shard_map/ppermute | solution.py:362
  3.7 33.4 %collective-permute-start.2 = (f32[20,8,1024]{2,1,0:T(8,128)S(1)}, f32[20,8,1024]{2,1,0:T(8,128)S(1)}, u32[]{:S(2)}, u32[]{:S(2)}) collective-permute-start(f32[20,8,1024]{2,1,0:T(8,128)S(1)} %get-tuple-element.19), channel_id=1, source_target_pairs={{16,0},{17,1},{18,2},{19,3},{20,4},{21,5},{22,6},{23,7},{24,8},{25... | collective-permute-start | bytes 1966088 | tf_op jit(solution)/shard_map/ppermute | solution.py:362
  6.4 30.7 %collective-permute-start.5 = (f32[10,8,1024]{2,1,0:T(8,128)S(1)}, f32[10,8,1024]{2,1,0:T(8,128)S(1)}, u32[]{:S(2)}, u32[]{:S(2)}) collective-permute-start(f32[10,8,1024]{2,1,0:T(8,128)S(1)} %collective-permute-done.4), channel_id=1, source_target_pairs={{305,241},{307,243},{452,244},{277,245},{454,246},{279,247},{328,2... | collective-permute-start | bytes 983048 | tf_op jit(solution)/shard_map/ppermute | solution.py:362
  7.1 30.0 %collective-permute-start.7 = (f32[10,8,1024]{2,1,0:T(8,128)S(1)}, f32[10,8,1024]{2,1,0:T(8,128)S(1)}, u32[]{:S(2)}, u32[]{:S(2)}) collective-permute-start(f32[10,8,1024]{2,1,0:T(8,128)S(1)} %collective-permute-done.6), channel_id=1, source_target_pairs={{465,241},{467,243},{372,244},{325,245},{374,246},{327,247},{280,2... | collective-permute-start | bytes 983048 | tf_op jit(solution)/shard_map/ppermute | solution.py:362
  7.8 4.7 %collective-permute-start = (f32[2,5,8,128]{3,2,1,0:T(8,128)S(1)}, f32[2,5,8,128]{3,2,1,0:T(8,128)S(1)}, u32[]{:S(2)}, u32[]{:S(2)}) collective-permute-start(f32[2,5,8,128]{3,2,1,0:T(8,128)S(1)} %get-tuple-element.15), channel_id=1, source_target_pairs={{1,0},{2,1},{3,2},{4,3},{5,4},{6,5},{7,6},{8,7},{9,8},{10,9},{11,1... | collective-permute-start | bytes 122888 | tf_op jit(solution)/shard_map/ppermute | solution.py:362
  10.2 5.3 %collective-permute-start.1 = (f32[2,5,8,128]{3,2,1,0:T(8,128)S(1)}, f32[2,5,8,128]{3,2,1,0:T(8,128)S(1)}, u32[]{:S(2)}, u32[]{:S(2)}) collective-permute-start(f32[2,5,8,128]{3,2,1,0:T(8,128)S(1)} %get-tuple-element.16), channel_id=1, source_target_pairs={{0,1},{1,2},{2,3},{3,4},{4,5},{5,6},{6,7},{7,8},{8,9},{9,10},{10,1... | collective-permute-start | bytes 122888 | tf_op jit(solution)/shard_map/ppermute | solution.py:362
  15.6 21.5 %collective-permute-start.3 = (f32[1,5,8,128]{3,2,1,0:T(8,128)S(1)}, f32[1,5,8,128]{3,2,1,0:T(8,128)S(1)}, u32[]{:S(2)}, u32[]{:S(2)}) collective-permute-start(f32[1,5,8,128]{3,2,1,0:T(8,128)S(1)} %slice.4), channel_id=1, source_target_pairs={{16,0},{17,1},{18,2},{19,3},{20,4},{21,5},{22,6},{23,7},{24,8},{25... | collective-permute-start | bytes 61448 | tf_op jit(solution)/shard_map/ppermute | solution.py:362

commit v6 on v5

--- a/solution.py
+++ b/solution.py
@@ -27,8 +27,8 @@
 COLUMN_SETS = (
     (None, ((3, 0), (1, 3))),
     (((0, 3), (3, 1)), ((1, 0), (0, 1))),
-    (((0, 1), (1, 0)), ((2, 0), (0, 3))),
-    (((0, 2), (3, 0)), ((1, 1), (2, 0))),
+    (((1, 1), (0, 3)), ((0, 2), (1, 2))),
+    (((0, 1), (3, 0)), ((2, 0), (0, 2))),
 )
 SOURCE_XY = (0, 0)
 TARGET_XY = (3, 3)
@@ -72,9 +72,12 @@
     return n, unit - STARTS[n]
 
 
-def masked_tile(buf, first, stop, d, q, j, base):
+def valid_rows(first, stop, d, q):
     row = AZ * (lax.broadcasted_iota(jnp.int32, (8, LANES), 0) % LOOKS) + q
-    keep = (row >= first[d]) & (row < stop[d])
+    return (row >= first[d]) & (row < stop[d])
+
+
+def masked_tile(buf, keep, q, j, base):
     at = base + q * ROW + 2 * j
     tile = jnp.concatenate(
         [buf[pl.ds(at + part, LOOKS, stride=AZ * ROW), :] for part in range(2)], axis=0
@@ -105,11 +108,12 @@
         copies[d].wait()
         slot = d % LAG
         for q in range(AZ):
+            keep = valid_rows(first, stop, d, q)
             for j in range(CHUNKS):
                 is_edge = j in (0, CHUNKS - 1)
                 if d >= LAG and not is_edge:
                     continue
-                tile = masked_tile(buf, first, stop, d, q, j, d * PER_DATE)
+                tile = masked_tile(buf, keep, q, j, d * PER_DATE)
                 if d < LAG:
                     n, at = place(d * AZ + q)
                     lanes = slice(j * LANES, (j + 1) * LANES)
@@ -127,9 +131,10 @@
     for d in range(LAG, DATES):
         copies[d - LAG].wait()
         for q in range(AZ):
+            keep = valid_rows(first, stop, d, q)
             for j in range(CHUNKS):
                 high[d - LAG, q, :, j * LANES : (j + 1) * LANES] = masked_tile(
-                    buf, first, stop, d, q, j, (d - LAG) * PER_DATE
+                    buf, keep, q, j, (d - LAG) * PER_DATE
                 )
 
 
@@ -179,11 +184,10 @@
         )
 
 
-def windows(sums, g):
+def windows(left):
     k = lax.broadcasted_iota(jnp.int32, (2 * GROUP, GROUP), 0) - LANES
     n = lax.broadcasted_iota(jnp.int32, (2 * GROUP, GROUP), 1)
     band = ((k >= n - MARGIN) & (k < n + MARGIN)).astype(jnp.float32).astype(jnp.bfloat16)
-    left = sums[:, g * GROUP : (g + 2) * GROUP]
     total = None
     for _ in range(3):
         term = left.astype(jnp.bfloat16)
@@ -241,14 +245,14 @@
     )
     for g in range(COLS // GROUP):
         lanes = slice(g * GROUP, (g + 1) * GROUP)
-        result = windows(sums, g)
+        result = windows(sums[:, g * GROUP : (g + 2) * GROUP])
         powers = unpacked_powers(result, 8 * len(INNER_PAIRS), DATES)
         for d in range(OUTER_FIRST, DATES):
             power[d - OUTER_FIRST, :, lanes] = powers[d]
         for n, (i, k) in enumerate(INNER_PAIRS):
 
             def store(m, value, i=i, k=k, lanes=lanes):
-                out[i, k, m, :, lanes] = value
+                out[i * LAG + k, m, :, lanes] = value
 
             write_pair(
                 store,
@@ -259,18 +263,52 @@
             )
 
 
-def outer(*refs):
+def write_outer(result, power, used, staged, at, lanes):
+    powers = unpacked_powers(result, 8 * len(OUTER_PAIRS), LAG)
+    for n, (i, k) in enumerate(OUTER_PAIRS):
+
+        def store(m, value, n=n):
+            staged[n, m, :, at : at + GROUP] = value
+
+        write_pair(
+            store,
+            result[8 * n : 8 * n + 8],
+            power[i - OUTER_FIRST, :, lanes],
+            powers[i + k + 1 - DATES],
+            used[k, i].astype(jnp.float32),
+        )
+
+
+def copies_out(staged, out, sems, parts):
+    where = [i * LAG + k for i, k in OUTER_PAIRS]
+    heads = [n for n in range(len(where)) if n == 0 or where[n] != where[n - 1] + 1]
+    copies = []
+    for (at, lane), sem in zip(parts, range(len(parts))):
+        width = 2 * GROUP // len(parts)
+        for head, following in zip(heads, heads[1:] + [len(where)]):
+            size = following - head
+            copies.append(
+                pltpu.make_async_copy(
+                    staged.at[pl.ds(head, size), :, :, pl.ds(at, width)],
+                    out.at[pl.ds(where[head], size), :, :, pl.ds(lane, width)],
+                    sems.at[sem, heads.index(head)],
+                )
+            )
+    for copy in copies:
+        copy.start()
+    return copies
+
+
+def outer_middle(*refs):
     pieces = refs[:COUNT]
-    high, edges, power, used, received, their_edges = refs[COUNT : COUNT + 6]
-    far = refs[COUNT + 6 : 2 * COUNT + 6]
-    out, sums, staged, sems = refs[2 * COUNT + 7 :]
+    high, power, used, received = refs[COUNT : COUNT + 4]
+    far = refs[COUNT + 4 : 2 * COUNT + 4]
+    out, sums, staged, sems = refs[2 * COUNT + 5 :]
     dates = range(OUTER_FIRST, DATES)
 
-    def body(tiles, lanes):
-        mine, theirs = tiles
-        look_sums(sums, OUTER_PAIRS, DATES, mine, theirs, theirs, lanes)
-
-    def tiles_at(lanes):
+    @pl.loop(0, CHUNKS)
+    def _(c):
+        lanes = pl.ds(pl.multiple_of(c * LANES, LANES), LANES)
         theirs = []
         for d in range(LAG):
             units = [d * AZ + q for q in range(AZ)]
@@ -280,39 +318,37 @@
                     for unit in units
                 ]
             )
-        return own_tiles(pieces, high, lanes, dates), theirs
-
-    fill(
-        sums,
-        tiles_at,
+        mine = own_tiles(pieces, high, lanes, dates)
+        look_sums(sums, OUTER_PAIRS, DATES, mine, theirs, theirs, lanes)
+
+    for g in (1, 2):
+        lanes = slice(g * GROUP, (g + 1) * GROUP)
+        result = windows(sums[:, g * GROUP - LANES : (g + 2) * GROUP - LANES])
+        write_outer(result, power, used, staged, (g - 1) * GROUP, lanes)
+    for copy in copies_out(staged, out, sems, [(0, GROUP)]):
+        copy.wait()
+
+
+def outer_sides(sums, edges, power, used, their_edges, out_in, out, halo, staged, sems):
+    del out_in
+    dates = range(OUTER_FIRST, DATES)
+    mine = {d: halo_of(edges, d) for d in dates}
+    theirs = [halo_of(their_edges, d) for d in range(LAG)]
+    look_sums(halo, OUTER_PAIRS, DATES, mine, theirs, theirs, slice(0, LANES))
+    ends = halo[...]
+    inside = 2 * GROUP - LANES
+    copies = []
+    for part, left in enumerate(
         (
-            {d: halo_of(edges, d) for d in dates},
-            [halo_of(their_edges, d) for d in range(LAG)],
-        ),
-        body,
-    )
-    for g in range(COLS // GROUP):
-        lanes = slice(g * GROUP, (g + 1) * GROUP)
-        result = windows(sums, g)
-        powers = unpacked_powers(result, 8 * len(OUTER_PAIRS), LAG)
-        for n, (i, k) in enumerate(OUTER_PAIRS):
-
-            def store(m, value, n=n, lanes=lanes):
-                staged[n, m, :, lanes] = value
-
-            write_pair(
-                store,
-                result[8 * n : 8 * n + 8],
-                power[i - OUTER_FIRST, :, lanes],
-                powers[i + k + 1 - DATES],
-                used[k, i].astype(jnp.float32),
-            )
-    copies = [
-        pltpu.make_async_copy(staged.at[n], out.at[i, k], sems.at[n])
-        for n, (i, k) in enumerate(OUTER_PAIRS)
-    ]
-    for copy in copies:
-        copy.start()
+            jnp.concatenate([ends, sums[:, :inside]], axis=1),
+            jnp.concatenate([sums[:, COLS - inside :], ends], axis=1),
+        )
+    ):
+        lane = part * (COLS - GROUP)
+        write_outer(
+            windows(left), power, used, staged, part * GROUP, slice(lane, lane + GROUP)
+        )
+    copies = copies_out(staged, out, sems, [(0, 0), (GROUP, COLS - GROUP)])
     for copy in copies:
         copy.wait()
 
@@ -378,7 +414,7 @@
     their_edges = permute(edges[:1], near + far)
 
     used = pair_used.T
-    out_shape = f32(DATES, LAG, 3, LOOKS, COLS)
+    out_shape = f32(DATES * LAG, 3, LOOKS, COLS)
     out, power, high = pl.pallas_call(
         inner,
         out_shape=[
@@ -396,20 +432,33 @@
         compiler_params=PARAMS,
         name="inner",
     )(*pieces, in_hbm(slc), in_hbm(first_row), in_hbm(stop_row), edges, in_hbm(used))
-    return pl.pallas_call(
-        outer,
+    rows = sum_rows(OUTER_PAIRS, LAG)
+    scratch = pltpu.VMEM((len(OUTER_PAIRS), 3, LOOKS, 2 * GROUP), jnp.float32)
+    out, sums = pl.pallas_call(
+        outer_middle,
+        out_shape=[out_shape, f32_vmem(rows, COLS)],
+        in_specs=[VMEM] * (COUNT + 2) + [SMEM] + [VMEM] * (COUNT + 1) + [ANY],
+        out_specs=[ANY, VMEM],
+        input_output_aliases={2 * COUNT + 4: 0},
+        scratch_shapes=[scratch, pltpu.SemaphoreType.DMA((1, 3))],
+        compiler_params=PARAMS,
+        name="outer_middle",
+    )(*pieces, high, power, in_hbm(used), received, *gathered, out)
+    out = pl.pallas_call(
+        outer_sides,
         out_shape=out_shape,
-        in_specs=[VMEM] * (COUNT + 3) + [SMEM] + [VMEM] * (COUNT + 2) + [ANY],
+        in_specs=[VMEM] * 3 + [SMEM, VMEM, ANY],
         out_specs=ANY,
-        input_output_aliases={2 * COUNT + 6: 0},
+        input_output_aliases={5: 0},
         scratch_shapes=[
-            pltpu.VMEM((sum_rows(OUTER_PAIRS, LAG), WIDE), jnp.float32),
-            pltpu.VMEM((len(OUTER_PAIRS), 3, LOOKS, COLS), jnp.float32),
-            pltpu.SemaphoreType.DMA((len(OUTER_PAIRS),)),
+            pltpu.VMEM((rows, LANES), jnp.float32),
+            scratch,
+            pltpu.SemaphoreType.DMA((2, 3)),
         ],
         compiler_params=PARAMS,
-        name="outer",
-    )(*pieces, high, edges, power, in_hbm(used), received, their_edges, *gathered, out)
+        name="outer_sides",
+    )(sums, edges, power, in_hbm(used), their_edges, out)
+    return out.reshape(DATES, LAG, 3, LOOKS, COLS)
 
 
 def solution(mesh):

time: 40.3 us -> 39.9 us (0.990)
  the two profiles are of different devices: /device:TPU:62 before, /device:TPU:94 now
where the time goes in v6:
time: 39.9 us; the launch traced here: 39.6 us
  waiting for transfers between devices  15.8 us (40%)
  starting transfers between devices  13 us (33%)
  Pallas kernels  10.7 us (27%)
    ppermute x8, waiting for transfers between devices, permute(): return lax.ppermute(value, AXES, pairs)  15.8 us
    ppermute x8, starting transfers between devices, permute(): return lax.ppermute(value, AXES, pairs)  13 us
    pallas_call x1, Pallas kernels, on_device(): pl.pallas_call(inner, out_shape=[out_shape, f32_vmem(DATES - OUTER_FIRST,...  4.22 us
    pallas_call x1, Pallas kernels, on_device(): pl.pallas_call(outer_middle, out_shape=[out_shape, f32_vmem(rows, COLS)],...  2.3 us
    pallas_call x1, Pallas kernels, on_device(): pl.pallas_call(prepare, out_shape=piece_shapes + [f32_vmem(LAG * AZ, 8, C...  2.23 us
    pallas_call x1, Pallas kernels, on_device(): pl.pallas_call(outer_sides, out_shape=out_shape, in_specs=[VMEM] * 3 + [S...  1.9 us
  transfers between devices with their start and end apart: 8, of which 3 were waited for; matrix products, arithmetic and copies ran while one was open for 0% of the time, Pallas kernels for 16%

profile of v6, /device:TPU:94, one launch (start us, length us, event | category | flops | bytes accessed | tf_op | source)
XLA Modules:
  0.0 39.6 jit_solution(7723669442450532083)
XLA Ops:
  0.0 2.2 %prepare.1 = (f32[10,8,1024]{2,1,0:T(8,128)S(1)}, f32[10,8,1024]{2,1,0:T(8,128)S(1)}, f32[20,8,1024]{2,1,0:T(8,128)S(1)}, f32[2,5,8,128]{3,2,1,0:T(8,128)S(1)}, f32[2,5,8,128]{3,2,1,0:T(8,128)S(1)}) custom-call(f32[1920,128]{1,0:T(8,128)} %bitcast.7, s32[6]{0:T(128)} %refs_3_.1, s32[6]{0:T(128)} %refs_4_.1), custom_call_target="tpu_custom_call" | custom-call | tf_op jit(solution)/shard_map/prepare/pallas_call | solution.py:384
  2.2 0.7 %collective-permute-start.3 = (f32[10,8,1024]{2,1,0:T(8,128)S(1)}, f32[10,8,1024]{2,1,0:T(8,128)S(1)}, u32[]{:S(2)}, u32[]{:S(2)}) collective-permute-start(f32[10,8,1024]{2,1,0:T(8,128)S(1)} %get-tuple-element.15.refs_0_), channel_id=1, source_target_pairs={{257,305},{259,307},{260,452},{261,277},{262,454},{263,279},{264,3... | collective-permute-start | bytes 983048 | tf_op jit(solution)/shard_map/ppermute | solution.py:398
  2.9 0.7 %collective-permute-start.5 = (f32[10,8,1024]{2,1,0:T(8,128)S(1)}, f32[10,8,1024]{2,1,0:T(8,128)S(1)}, u32[]{:S(2)}, u32[]{:S(2)}) collective-permute-start(f32[10,8,1024]{2,1,0:T(8,128)S(1)} %get-tuple-element.16.refs_1_), channel_id=1, source_target_pairs={{257,465},{259,467},{260,372},{261,325},{262,374},{263,327},{264,4... | collective-permute-start | bytes 983048 | tf_op jit(solution)/shard_map/ppermute | solution.py:398
  3.6 2.8 %collective-permute-start.2 = (f32[20,8,1024]{2,1,0:T(8,128)S(1)}, f32[20,8,1024]{2,1,0:T(8,128)S(1)}, u32[]{:S(2)}, u32[]{:S(2)}) collective-permute-start(f32[20,8,1024]{2,1,0:T(8,128)S(1)} %get-tuple-element.21), channel_id=1, source_target_pairs={{16,0},{17,1},{18,2},{19,3},{20,4},{21,5},{22,6},{23,7},{24,8},{25... | collective-permute-start | bytes 1966088 | tf_op jit(solution)/shard_map/ppermute | solution.py:398
  6.4 0.0 collective-permute-done.3
  6.4 1.3 %collective-permute-start.4 = (f32[10,8,1024]{2,1,0:T(8,128)S(1)}, f32[10,8,1024]{2,1,0:T(8,128)S(1)}, u32[]{:S(2)}, u32[]{:S(2)}) collective-permute-start(f32[10,8,1024]{2,1,0:T(8,128)S(1)} %collective-permute-done.3), channel_id=1, source_target_pairs={{305,241},{307,243},{452,244},{277,245},{454,246},{279,247},{344,2... | collective-permute-start | bytes 983048 | tf_op jit(solution)/shard_map/ppermute | solution.py:398
  7.7 0.0 collective-permute-done.5
  7.7 1.3 %collective-permute-start.6 = (f32[10,8,1024]{2,1,0:T(8,128)S(1)}, f32[10,8,1024]{2,1,0:T(8,128)S(1)}, u32[]{:S(2)}, u32[]{:S(2)}) collective-permute-start(f32[10,8,1024]{2,1,0:T(8,128)S(1)} %collective-permute-done.5), channel_id=1, source_target_pairs={{465,241},{467,243},{372,244},{325,245},{374,246},{327,247},{456,2... | collective-permute-start | bytes 983048 | tf_op jit(solution)/shard_map/ppermute | solution.py:398
  9.0 1.9 %collective-permute-start = (f32[2,5,8,128]{3,2,1,0:T(8,128)S(1)}, f32[2,5,8,128]{3,2,1,0:T(8,128)S(1)}, u32[]{:S(2)}, u32[]{:S(2)}) collective-permute-start(f32[2,5,8,128]{3,2,1,0:T(8,128)S(1)} %get-tuple-element.17), channel_id=1, source_target_pairs={{1,0},{2,1},{3,2},{4,3},{5,4},{6,5},{7,6},{8,7},{9,8},{10,9},{11,1... | collective-permute-start | bytes 122888 | tf_op jit(solution)/shard_map/ppermute | solution.py:398
  11.0 2.4 %collective-permute-start.1 = (f32[2,5,8,128]{3,2,1,0:T(8,128)S(1)}, f32[2,5,8,128]{3,2,1,0:T(8,128)S(1)}, u32[]{:S(2)}, u32[]{:S(2)}) collective-permute-start(f32[2,5,8,128]{3,2,1,0:T(8,128)S(1)} %get-tuple-element.18), channel_id=1, source_target_pairs={{0,1},{1,2},{2,3},{3,4},{4,5},{5,6},{6,7},{7,8},{8,9},{9,10},{10,1... | collective-permute-start | bytes 122888 | tf_op jit(solution)/shard_map/ppermute | solution.py:398
  13.4 0.0 collective-permute-done
  13.4 2.9 %collective-permute-done.1 = f32[2,5,8,128]{3,2,1,0:T(8,128)S(1)} collective-permute-done((f32[2,5,8,128]{3,2,1,0:T(8,128)S(1)}, f32[2,5,8,128]{3,2,1,0:T(8,128)S(1)}, u32[]{:S(2)}, u32[]{:S(2)}) %collective-permute-start.1) | collective-permute-done | bytes 40992 | tf_op jit(solution)/shard_map/ppermute | solution.py:398
  16.3 1.9 %collective-permute-start.7 = (f32[1,5,8,128]{3,2,1,0:T(8,128)S(1)}, f32[1,5,8,128]{3,2,1,0:T(8,128)S(1)}, u32[]{:S(2)}, u32[]{:S(2)}) collective-permute-start(f32[1,5,8,128]{3,2,1,0:T(8,128)S(1)} %slice.4), channel_id=1, source_target_pairs={{16,0},{17,1},{18,2},{19,3},{20,4},{21,5},{22,6},{23,7},{24,8},{25... | collective-permute-start | bytes 61448 | tf_op jit(solution)/shard_map/ppermute | solution.py:398
  18.2 4.2 %inner.1 = (f32[24,3,4,1024]{3,2,1,0:T(4,128)}, f32[4,8,1024]{2,1,0:T(8,128)S(1)}, f32[2,5,8,1024]{3,2,1,0:T(8,128)S(1)}) custom-call(f32[10,8,1024]{2,1,0:T(8,128)S(1)} %get-tuple-element.15.refs_0_, f32[10,8,1024]{2,1,0:T(8,128)S(1)} %get-tuple-element.16.refs_1_, f32[1920,128]{1,0:T(8,128)} %bitcast.8, s32[6]{0:T(128)} %refs_3_.1, s32[6]{0:T(128)} %refs_4_.1, ...), custom_call_target="tpu_custom_call" | custom-call | tf_op jit(solution)/shard_map/inner/pallas_call | solution.py:418
  22.4 8.4 %collective-permute-done.4.refs_6_ = f32[10,8,1024]{2,1,0:T(8,128)S(1)} collective-permute-done((f32[10,8,1024]{2,1,0:T(8,128)S(1)}, f32[10,8,1024]{2,1,0:T(8,128)S(1)}, u32[]{:S(2)}, u32[]{:S(2)}) %collective-permute-start.4) | collective-permute-done | bytes 327712 | tf_op jit(solution)/shard_map/ppermute | solution.py:398
  30.9 4.5 %collective-permute-done.6.refs_7_ = f32[10,8,1024]{2,1,0:T(8,128)S(1)} collective-permute-done((f32[10,8,1024]{2,1,0:T(8,128)S(1)}, f32[10,8,1024]{2,1,0:T(8,128)S(1)}, u32[]{:S(2)}, u32[]{:S(2)}) %collective-permute-start.6) | collective-permute-done | bytes 327712 | tf_op jit(solution)/shard_map/ppermute | solution.py:398
  35.4 0.0 collective-permute-done.2.refs_5_
  35.4 2.3 %outer_middle.1 = (f32[24,3,4,1024]{3,2,1,0:T(4,128)}, f32[96,1024]{1,0:T(8,128)S(1)}) custom-call(f32[10,8,1024]{2,1,0:T(8,128)S(1)} %get-tuple-element.15.refs_0_, f32[10,8,1024]{2,1,0:T(8,128)S(1)} %get-tuple-element.16.refs_1_, f32[2,5,8,1024]{3,2,1,0:T(8,128)S(1)} %get-tuple-element.19.refs_2_, ...), custom_call_target="tpu_custom_call", output_to_operand_aliasing={{0}: (8, {})} | custom-call | tf_op jit(solution)/shard_map/outer_middle/pallas_call | solution.py:437
  37.7 0.0 collective-permute-done.7.their_edges
  37.7 1.9 %outer_sides.1 = f32[24,3,4,1024]{3,2,1,0:T(4,128)} custom-call(f32[96,1024]{1,0:T(8,128)S(1)} %get-tuple-element.23.sums, f32[2,5,8,128]{3,2,1,0:T(8,128)S(1)} %add.3.refs_5_.edges, f32[4,8,1024]{2,1,0:T(8,128)S(1)} %get-tuple-element.20.refs_3_.power, s32[4,6]{1,0:T(4,128)} %bitcast.11, ...), custom_call_target="tpu_custom_call", output_to_operand_aliasing={{}: (5, {})} | custom-call | tf_op jit(solution)/shard_map/outer_sides/pallas_call | solution.py:447
  (2 shorter events, 0.0 us)
Async XLA Ops:
  2.2 4.2 %collective-permute-start.3 = (f32[10,8,1024]{2,1,0:T(8,128)S(1)}, f32[10,8,1024]{2,1,0:T(8,128)S(1)}, u32[]{:S(2)}, u32[]{:S(2)}) collective-permute-start(f32[10,8,1024]{2,1,0:T(8,128)S(1)} %get-tuple-element.15.refs_0_), channel_id=1, source_target_pairs={{257,305},{259,307},{260,452},{261,277},{262,454},{263,279},{264,3... | collective-permute-start | bytes 983048 | tf_op jit(solution)/shard_map/ppermute | solution.py:398
  2.9 4.8 %collective-permute-start.5 = (f32[10,8,1024]{2,1,0:T(8,128)S(1)}, f32[10,8,1024]{2,1,0:T(8,128)S(1)}, u32[]{:S(2)}, u32[]{:S(2)}) collective-permute-start(f32[10,8,1024]{2,1,0:T(8,128)S(1)} %get-tuple-element.16.refs_1_), channel_id=1, source_target_pairs={{257,465},{259,467},{260,372},{261,325},{262,374},{263,327},{264,4... | collective-permute-start | bytes 983048 | tf_op jit(solution)/shard_map/ppermute | solution.py:398
  3.6 31.7 %collective-permute-start.2 = (f32[20,8,1024]{2,1,0:T(8,128)S(1)}, f32[20,8,1024]{2,1,0:T(8,128)S(1)}, u32[]{:S(2)}, u32[]{:S(2)}) collective-permute-start(f32[20,8,1024]{2,1,0:T(8,128)S(1)} %get-tuple-element.21), channel_id=1, source_target_pairs={{16,0},{17,1},{18,2},{19,3},{20,4},{21,5},{22,6},{23,7},{24,8},{25... | collective-permute-start | bytes 1966088 | tf_op jit(solution)/shard_map/ppermute | solution.py:398
  6.4 24.5 %collective-permute-start.4 = (f32[10,8,1024]{2,1,0:T(8,128)S(1)}, f32[10,8,1024]{2,1,0:T(8,128)S(1)}, u32[]{:S(2)}, u32[]{:S(2)}) collective-permute-start(f32[10,8,1024]{2,1,0:T(8,128)S(1)} %collective-permute-done.3), channel_id=1, source_target_pairs={{305,241},{307,243},{452,244},{277,245},{454,246},{279,247},{344,2... | collective-permute-start | bytes 983048 | tf_op jit(solution)/shard_map/ppermute | solution.py:398
  7.7 27.6 %collective-permute-start.6 = (f32[10,8,1024]{2,1,0:T(8,128)S(1)}, f32[10,8,1024]{2,1,0:T(8,128)S(1)}, u32[]{:S(2)}, u32[]{:S(2)}) collective-permute-start(f32[10,8,1024]{2,1,0:T(8,128)S(1)} %collective-permute-done.5), channel_id=1, source_target_pairs={{465,241},{467,243},{372,244},{325,245},{374,246},{327,247},{456,2... | collective-permute-start | bytes 983048 | tf_op jit(solution)/shard_map/ppermute | solution.py:398
  9.0 4.3 %collective-permute-start = (f32[2,5,8,128]{3,2,1,0:T(8,128)S(1)}, f32[2,5,8,128]{3,2,1,0:T(8,128)S(1)}, u32[]{:S(2)}, u32[]{:S(2)}) collective-permute-start(f32[2,5,8,128]{3,2,1,0:T(8,128)S(1)} %get-tuple-element.17), channel_id=1, source_target_pairs={{1,0},{2,1},{3,2},{4,3},{5,4},{6,5},{7,6},{8,7},{9,8},{10,9},{11,1... | collective-permute-start | bytes 122888 | tf_op jit(solution)/shard_map/ppermute | solution.py:398
  11.0 5.3 %collective-permute-start.1 = (f32[2,5,8,128]{3,2,1,0:T(8,128)S(1)}, f32[2,5,8,128]{3,2,1,0:T(8,128)S(1)}, u32[]{:S(2)}, u32[]{:S(2)}) collective-permute-start(f32[2,5,8,128]{3,2,1,0:T(8,128)S(1)} %get-tuple-element.18), channel_id=1, source_target_pairs={{0,1},{1,2},{2,3},{3,4},{4,5},{5,6},{6,7},{7,8},{8,9},{9,10},{10,1... | collective-permute-start | bytes 122888 | tf_op jit(solution)/shard_map/ppermute | solution.py:398
  16.3 21.4 %collective-permute-start.7 = (f32[1,5,8,128]{3,2,1,0:T(8,128)S(1)}, f32[1,5,8,128]{3,2,1,0:T(8,128)S(1)}, u32[]{:S(2)}, u32[]{:S(2)}) collective-permute-start(f32[1,5,8,128]{3,2,1,0:T(8,128)S(1)} %slice.4), channel_id=1, source_target_pairs={{16,0},{17,1},{18,2},{19,3},{20,4},{21,5},{22,6},{23,7},{24,8},{25... | collective-permute-start | bytes 61448 | tf_op jit(solution)/shard_map/ppermute | solution.py:398
